TPU v7x, 128 devices: a whole 4x4x4 slice. The times are simulated.
128 devices in a mesh: row: 8 (over y, x_hi), col: 16 (over x_lo, z, core).
Axes of the slice: x: 4 (x_hi: 2, x_lo: 2; x = x_hi * 2 + x_lo), y: 4, z: 4, core: 2. Of those that a mesh axis runs over, the one named last changes fastest.
Arguments:
- a_blocks: float32 [8, 16, 4, 128, 128], P('row', 'col'), may hold values from -1.2 to 1.2
- a_index: int32 [8, 16, 4], P('row', 'col'), may hold values from -1 to 63, as said below
- b_blocks: float32 [8, 16, 2, 8, 128, 128], P('row', 'col'), may hold values from -1.2 to 1.2
- b_index: int32 [8, 16, 2, 8], P('row', 'col'), may hold values from -1 to 63, as said below
- c_index: int32 [8, 16, 16], P('row', 'col'), may hold values from -1 to 63, as said below
Outputs:
- c_blocks: float32 [8, 16, 16, 128, 128], P('row', 'col')
Inputs may be any that keep to these rules, and one draw needn't show every extreme that they name: `a_index`: within each tile the non-negative entries are distinct and come before the entries -1, which mark empty slots; every tile has at least one block and some tile has all 4 slots filled. `b_index`: within each panel of a device the non-negative entries are distinct and come before the entries -1, which mark empty slots; every panel has at least one block and some panel has all 8 slots filled. `c_index`: within each tile the non-negative entries are distinct and come before the entries -1, which mark empty slots; every tile keeps at least one block and some tile has all 16 slots filled.
All inputs are finite; a program needn't handle non-finite values.
Results may differ from a plain program's by a relative error of at most 0.0003.
Values sent between devices are 32-bit elements; how exact they have to be, the bound alone decides.
No kernel may reach another device: no remote copies, remote signals or barrier semaphores. Data moves between devices by JAX's collectives and lax.ppermute only.
A program may use at most 192 MiB of HBM per device.

v0:
```python
import functools

import jax
import jax.numpy as jnp
from jax import lax
from jax.experimental import pallas as pl
from jax.experimental.pallas import tpu as pltpu
from jax.sharding import Mesh
from jax.sharding import PartitionSpec as P

SA = 4
PK = 8
NBD = 8
NEAR = 6
FAR = 3
COL = ("x_lo", "z", "core")
VMEM_LIMIT = 8 << 20
A_PARTS = 8
LIST = 512
AHEAD = 8


def matmul(a, b):
    return jnp.dot(a.astype(jnp.bfloat16), b, preferred_element_type=jnp.float32)


def lands_at(a_line, b):
    meet = (a_line >= 0) & (b >= 0) & ((a_line & (PK - 1)) == (b >> 3))
    return jnp.where(meet, (a_line >> 3) * NBD + (b & (NBD - 1)), -2)


def needed(a, b, c):
    need = jnp.zeros(b.shape, jnp.bool_)
    for s in range(SA):
        lands = lands_at(a[s : s + 1], b)
        for n in range(c.shape[0]):
            need = need | (lands == c[n : n + 1])
    return need


def lane_facts(shape, axis=1):
    lane = lax.broadcasted_iota(jnp.int32, shape, axis)
    r, p = lane >> 4, lane & 15
    owner = p >> 1
    far = (((owner >> 1) - (r >> 1)) & 3) == 2
    way = ((owner ^ r) & 1) + jnp.where(far, 2, 0)
    return r, p, owner, way


def code(a_slot, part, at, c_slot):
    return ((a_slot * 16 + part) * 128 + at) * 16 + c_slot


def a_of(word):
    return word >> 15


def part_of(word):
    return (word >> 11) & 15


def at_of(word):
    return (word >> 4) & 127


def c_of(word):
    return word & 15


def fetch_a(word, a_refs, dst, sem):
    a = a_of(word)
    fetch_block(a >> 3, a & 7, a_refs, dst, sem)


def fetch_block(part, at, refs, dst, sem):
    for i, ref in enumerate(refs):

        def start(ref=ref):
            pltpu.make_async_copy(ref.at[at], dst, sem).start()

        if len(refs) == 1:
            start()
        else:
            pl.when(part == i)(start)


def make_maps(maps_ref):
    shape = maps_ref.shape[1:]
    lane = lax.broadcasted_iota(jnp.int32, shape, 1)
    down = lax.broadcasted_iota(jnp.int32, shape, 0)
    r, p, owner, way = lane_facts(shape)
    r_down, p_down, _, way_down = lane_facts(shape, 0)
    holder = (p_down == 0) & (r_down == owner)
    alike = (r == r_down) & (way == way_down)
    y, xh, xl, z, core = lane >> 5, (lane >> 4) & 1, (lane >> 3) & 1, (lane >> 1) & 3, lane & 1
    listed_at = (((core * 2 + xh) * 2 + xl) * 4 + z) * 4 + y
    for n, flags in enumerate(
        [
            holder & ((p & 1) == 0),
            holder & ((p & 1) == 1),
            (p_down == 0) & (r == r_down),
            alike,
            alike & (down < lane),
            down == listed_at,
        ]
    ):
        maps_ref[n] = jnp.where(flags, 1.0, 0.0).astype(jnp.bfloat16)


def positions(spots_ref, maps_ref):
    spots = spots_ref[...].astype(jnp.float32).astype(jnp.bfloat16)
    return lax.dot_general(
        spots, maps_ref[5], (((0,), (0,)), ((), ())), preferred_element_type=jnp.float32
    )


def list_sends(sends, row, order, turn, pack_list):
    r, p, owner, _ = lane_facts(order.shape)
    t = lax.broadcasted_iota(jnp.int32, order.shape, 0)
    steps = ((owner >> 1) - (row >> 1)) & 3
    part = jnp.where(steps == 0, 0, jnp.where(steps == 3, 1, 2))
    word = (part * 16 + (p & 1) * 8 + t).astype(jnp.float32)
    n = 0
    for slots, which, there in sends:
        for e in range(slots):
            hit = (order == which * 128 + turn * slots + e) & (r == there(row))
            pack_list[n] = jnp.max(jnp.where(hit, word, -1.0)).astype(jnp.int32)
            n += 1


def relist_kernel(sends, me_ref, turn_ref, info_ref, pack_list):
    list_sends(sends, me_ref[0], info_ref[32:40], turn_ref[0], pack_list)


def relist(me, turn, info, sends):
    smem = pl.BlockSpec(memory_space=pltpu.SMEM)
    return pl.pallas_call(
        functools.partial(relist_kernel, sends),
        in_specs=[smem, smem, pl.BlockSpec(memory_space=pltpu.VMEM)],
        out_specs=smem,
        out_shape=jax.ShapeDtypeStruct((sum(n for n, *_ in sends),), jnp.int32),
        compiler_params=pltpu.CompilerParams(vmem_limit_bytes=4 << 20),
        name="relist",
    )(me, turn, info)


def plan_kernel(sends, me_ref, spots_ref, pack_list, info_ref, maps_ref):
    row, column = me_ref[0], me_ref[1]
    make_maps(maps_ref)
    held = positions(spots_ref, maps_ref)
    a = held[:8].astype(jnp.int32)
    turned = pltpu.roll(held[8:40], (128 - column) & 127, 1)
    b = matmul(turned[:8], maps_ref[0]) + matmul(turned[8:16], maps_ref[1])
    b = b.astype(jnp.int32)
    c = matmul(turned[16:32], maps_ref[2]).astype(jnp.int32)
    need = needed(a, b, c)

    r, p, owner, way = lane_facts(b.shape)
    t = lax.broadcasted_iota(jnp.int32, b.shape, 0)
    flags = jnp.where(need, 1.0, 0.0)
    alike = matmul(flags, maps_ref[3])
    upto = alike
    for step in (1, 2, 4):
        upto = upto + jnp.where(t >= step, pltpu.roll(upto, step, 0), 0.0)
    rank = (upto - alike + matmul(flags, maps_ref[4])).astype(jnp.int32)
    order = jnp.where(need, way * 128 + rank, -1)

    list_sends(sends, row, order, 0, pack_list)
    info_ref[0:8] = a
    info_ref[8:16] = b
    info_ref[16:32] = c
    info_ref[32:40] = order


def plan(me, spots, sends):
    smem = pl.BlockSpec(memory_space=pltpu.SMEM)
    vmem = pl.BlockSpec(memory_space=pltpu.VMEM)
    return pl.pallas_call(
        functools.partial(plan_kernel, sends),
        in_specs=[smem, vmem],
        out_specs=[smem, vmem, vmem],
        out_shape=[
            jax.ShapeDtypeStruct((sum(n for n, *_ in sends),), jnp.int32),
            jax.ShapeDtypeStruct((40, 128), jnp.int32),
            jax.ShapeDtypeStruct((6, 128, 128), jnp.bfloat16),
        ],
        compiler_params=pltpu.CompilerParams(vmem_limit_bytes=4 << 20),
        name="plan",
    )(me, spots)


def pack_kernel(sizes, list_ref, *rest):
    near, packed, sems = rest[:3], rest[3:-1], rest[-1]
    places = [(i, e) for i, size in enumerate(sizes) for e in range(size)]
    for n, (i, e) in enumerate(places):
        word = list_ref[n]

        @pl.when(word >= 0)
        def _():
            fetch_block(word >> 4, word & 15, near, packed[i].at[e], sems.at[n])

    for n, (i, e) in enumerate(places):

        @pl.when(list_ref[n] >= 0)
        def _():
            pltpu.make_async_copy(near[0].at[0], packed[i].at[e], sems.at[n]).wait()


def pack(listing, near, sizes):
    size = near[0].shape[-1]
    return pl.pallas_call(
        functools.partial(pack_kernel, sizes),
        in_specs=[pl.BlockSpec(memory_space=pltpu.SMEM)]
        + [pl.BlockSpec(memory_space=pl.ANY)] * 3,
        out_specs=[pl.BlockSpec(memory_space=pltpu.VMEM)] * len(sizes),
        scratch_shapes=[pltpu.SemaphoreType.DMA((sum(sizes),))],
        out_shape=[jax.ShapeDtypeStruct((n, size, size), jnp.float32) for n in sizes],
        compiler_params=pltpu.CompilerParams(vmem_limit_bytes=4 << 20),
        name="pack",
    )(listing, *near)


def overflow_kernel(
    me_ref, info_ref, spots_ref, maps_ref, over_ref, product_list, zeros_ref, zero, sem
):
    zero[...] = jnp.zeros_like(zero)
    stores = [pltpu.make_async_copy(zero, zeros_ref.at[c], sem.at[c]) for c in range(sem.shape[0])]
    for store in stores:
        store.start()
    extract(entries_of(info_ref, me_ref)[0], product_list)
    held = positions(spots_ref, maps_ref)
    a = held[:8].astype(jnp.int32)
    turned = [held[8:40]] + [pltpu.roll(held[8:40], 128 - q, 1) for q in range(1, 16)]
    b = matmul(jnp.concatenate([x[:8] for x in turned]), maps_ref[0])
    b = b + matmul(jnp.concatenate([x[8:16] for x in turned]), maps_ref[1])
    b = b.astype(jnp.int32)
    c = matmul(jnp.concatenate([x[16:32] for x in turned]), maps_ref[2]).astype(jnp.int32)
    flags = [
        jnp.where(needed(a, b[q * 8 : q * 8 + 8], c[q * 16 : q * 16 + 16]), 1.0, 0.0)
        for q in range(16)
    ]
    alike = matmul(jnp.concatenate(flags), maps_ref[3])
    most = jnp.sum(alike[:8], axis=0, keepdims=True)
    for q in range(1, 16):
        most = jnp.maximum(most, jnp.sum(alike[q * 8 : q * 8 + 8], axis=0, keepdims=True))
    *_, way = lane_facts(most.shape)
    slots = jnp.where(way == 0, 128, jnp.where(way == 1, NEAR, FAR))
    slots = slots.astype(jnp.float32)
    turns = sum(jnp.where(most > k * slots, 1.0, 0.0) for k in range(1, 17))
    over_ref[0] = jnp.max(turns).astype(jnp.int32)
    for store in stores:
        store.wait()


def overflow(me, info, spots, maps, slots, size):
    smem = pl.BlockSpec(memory_space=pltpu.SMEM)
    vmem = pl.BlockSpec(memory_space=pltpu.VMEM)
    return pl.pallas_call(
        overflow_kernel,
        in_specs=[smem, vmem, vmem, vmem],
        out_specs=[smem, smem, pl.BlockSpec(memory_space=pltpu.HBM)],
        out_shape=[
            jax.ShapeDtypeStruct((1,), jnp.int32),
            jax.ShapeDtypeStruct((LIST + 1,), jnp.int32),
            jax.ShapeDtypeStruct((slots, size, size), jnp.float32),
        ],
        scratch_shapes=[pltpu.VMEM((size, size), jnp.float32), pltpu.SemaphoreType.DMA((slots,))],
        compiler_params=pltpu.CompilerParams(vmem_limit_bytes=4 << 20),
        cost_estimate=pl.CostEstimate(flops=10**9, bytes_accessed=10**5, transcendentals=0),
        name="overflow",
    )(me, info, spots, maps)


def halves(x):
    high = x.astype(jnp.bfloat16)
    return high, (x - high.astype(jnp.float32)).astype(jnp.bfloat16)


def block_product(a, b):
    a_high, a_low = halves(a)
    b_high, b_low = halves(b)
    dot = functools.partial(jnp.dot, preferred_element_type=jnp.float32)
    return dot(a_high, b_high) + (dot(a_high, b_low) + dot(a_low, b_high))


def extract(entries, list_ref):
    def more(state):
        n, word, left = state
        list_ref[n] = word.astype(jnp.int32)
        left = jnp.where(left == word, -1.0, left)
        return n + 1, jnp.max(left), left

    n, *_ = lax.while_loop(
        lambda state: state[1] >= 0, more, (jnp.int32(0), jnp.max(entries), entries)
    )
    list_ref[LIST] = n


def entries_of(info_ref, me_ref, turn=1):
    row, column = me_ref[0], me_ref[1]
    b, c, order = info_ref[8:16], info_ref[16:32], info_ref[32:40]
    r, p, owner, way = lane_facts(b.shape)
    t = lax.broadcasted_iota(jnp.int32, b.shape, 0)
    rank = order & 127
    steps = ((owner >> 1) - (row >> 1)) & 3
    part = jnp.where(steps == 0, 0, jnp.where(steps == 3, 1, 2))
    slots = jnp.where(way == 1, NEAR, FAR)
    sent = (way > 0) & (rank < slots)
    at = rank - turn * slots
    later = (way > 0) & (at >= 0) & (at < slots)
    along = ((p >> 1) - (column >> 1)) & 3
    beside = ((p ^ column) >> 3) & 1
    a_part = jnp.where(along == 0, 0, jnp.where(along == 3, 1, jnp.where(along == 1, 2, 3)))
    a_at = (a_part + 4 * ((p ^ column) & 1)) * 8 + beside * SA
    found = [[], []]
    for s in range(SA):
        lands = lands_at(info_ref[s : s + 1], b)
        c_slot = jnp.full(b.shape, -1, jnp.int32)
        for n in range(c.shape[0]):
            c_slot = jnp.where(lands == c[n : n + 1], n, c_slot)
        live = (c_slot >= 0) & (r == row)
        a_slot = a_at + s
        at_hand = jnp.where(
            way == 0,
            code(a_slot, part, (p & 1) * 8 + t, c_slot),
            code(a_slot, 2 + way, rank, c_slot),
        )
        in_turn = code(a_slot, (way - 1) & 3, at, c_slot)
        found[0].append(jnp.where(live & ((way == 0) | sent), at_hand, -1).astype(jnp.float32))
        found[1].append(jnp.where(live & later, in_turn, -1).astype(jnp.float32))
    return [jnp.concatenate(x) for x in found]


def multiply_listed(list_ref, a_refs, b_refs, acc, a_buf, b_buf, a_sem, b_sem, meanwhile):
    count = list_ref[LIST]

    def fetch(n):
        slot = n % AHEAD
        word = list_ref[n]
        fetch_a(word, a_refs, a_buf.at[slot], a_sem.at[slot])
        fetch_block(part_of(word), at_of(word), b_refs, b_buf.at[slot], b_sem.at[slot])

    for n in range(AHEAD):

        @pl.when(n < count)
        def _():
            fetch(n)

    meanwhile()

    def step(n, carry):
        slot = n % AHEAD
        pltpu.make_async_copy(a_refs[0].at[0], a_buf.at[slot], a_sem.at[slot]).wait()
        pltpu.make_async_copy(b_refs[0].at[0], b_buf.at[slot], b_sem.at[slot]).wait()
        acc[c_of(list_ref[n])] += block_product(a_buf[slot], b_buf[slot])

        @pl.when(n + AHEAD < count)
        def _():
            fetch(n + AHEAD)

        return carry

    lax.fori_loop(0, count, step, 0)


def all_kernel(parts, list_ref, *rest):
    a_refs, b_refs = rest[:A_PARTS], rest[A_PARTS:parts]
    _, out_ref, acc, c_sem, touched, *buffers = rest[parts:]
    slots = acc.shape[0]

    def stored(c):
        return pltpu.make_async_copy(acc.at[c], out_ref.at[c], c_sem.at[c])

    def meanwhile():
        for c in range(slots):
            touched[c] = 0

        def mark(n, carry):
            touched[c_of(list_ref[n])] = 1
            return carry

        lax.fori_loop(0, list_ref[LIST], mark, 0)
        acc[...] = jnp.zeros_like(acc)

    multiply_listed(list_ref, a_refs, b_refs, acc, *buffers, meanwhile)
    for c in range(slots):
        pl.when(touched[c] == 1)(lambda c=c: stored(c).start())
    for c in range(slots):
        pl.when(touched[c] == 1)(lambda c=c: stored(c).wait())


def add_listed(list_ref, a_refs, b_refs, total_ref, out_ref, acc, c_sem, stage, *buffers):
    count = list_ref[LIST]

    def touched(was, act):
        def step(n, carry):
            c = c_of(list_ref[n])

            @pl.when(stage[c] == was)
            def _():
                stage[c] = was + 1
                act(c)

            return carry

        lax.fori_loop(0, count, step, 0)

    def fetched(c):
        return pltpu.make_async_copy(total_ref.at[c], acc.at[c], c_sem.at[c])

    def stored(c):
        return pltpu.make_async_copy(acc.at[c], out_ref.at[c], c_sem.at[c])

    for c in range(acc.shape[0]):
        stage[c] = 0

    def meanwhile():
        touched(0, lambda c: fetched(c).start())
        touched(1, lambda c: fetched(c).wait())

    multiply_listed(list_ref, a_refs, b_refs, acc, *buffers, meanwhile)
    touched(2, lambda c: stored(c).start())
    touched(3, lambda c: stored(c).wait())


def rest_kernel(parts, me_ref, turn_ref, info_ref, *rest):
    a_refs, b_refs = rest[:A_PARTS], rest[A_PARTS:parts]
    total_ref, out_ref, rest_list, *buffers = rest[parts:]
    extract(entries_of(info_ref, me_ref, turn_ref[0])[1], rest_list)
    add_listed(rest_list, a_refs, b_refs, total_ref, out_ref, *buffers)


def products(kernel, leading, a_parts, b_parts, total, slots, own_list=False):
    size = a_parts[0].shape[-1]
    parts = len(a_parts) + len(b_parts)
    smem = pl.BlockSpec(memory_space=pltpu.SMEM)
    vmem = pl.BlockSpec(memory_space=pltpu.VMEM)
    hbm = pl.BlockSpec(memory_space=pltpu.HBM)
    operands = [*leading, *a_parts, *b_parts] + ([] if total is None else [total])
    return pl.pallas_call(
        functools.partial(kernel, parts),
        in_specs=[smem if x.ndim == 1 else vmem for x in leading]
        + [pl.BlockSpec(memory_space=pl.ANY)] * parts
        + ([] if total is None else [hbm]),
        out_specs=hbm,
        out_shape=jax.ShapeDtypeStruct((slots, size, size), jnp.float32),
        scratch_shapes=([pltpu.SMEM((LIST + 1,), jnp.int32)] if own_list else [])
        + [
            pltpu.VMEM((slots, size, size), jnp.float32),
            pltpu.SemaphoreType.DMA((slots,)),
            pltpu.SMEM((slots,), jnp.int32),
            pltpu.VMEM((AHEAD, size, size), jnp.float32),
            pltpu.VMEM((AHEAD, size, size), jnp.float32),
            pltpu.SemaphoreType.DMA((AHEAD,)),
            pltpu.SemaphoreType.DMA((AHEAD,)),
        ],
        input_output_aliases={} if total is None else {len(operands) - 1: 0},
        compiler_params=pltpu.CompilerParams(vmem_limit_bytes=VMEM_LIMIT),
        cost_estimate=pl.CostEstimate(
            flops=8 * 3 * 2 * size**3, bytes_accessed=24 * size * size * 4, transcendentals=0
        ),
        name="products",
    )(*operands)


def to_row(block, rows, there):
    return lax.ppermute(block, "row", [(i, there(i)) for i in range(rows)])


def on_z(i):
    return (i & 9) | ((i + 2) & 6)


def back_z(i):
    return (i & 9) | ((i - 2) & 6)


def moved(block, there, columns):
    return lax.ppermute(block, COL, [(i, there(i)) for i in range(columns)])


def line_kernel(a_ref, b_ref, c_ref, blocks_ref, line_ref, tile_ref, sem):
    copy = pltpu.make_async_copy(blocks_ref, tile_ref, sem.at[0])
    copy.start()
    lane = lax.broadcasted_iota(jnp.int32, line_ref.shape, 1)
    line = jnp.full(line_ref.shape, -1, jnp.int32)
    for n in range(a_ref.shape[0]):
        line = jnp.where(lane == n, a_ref[n], line)
    for h in range(b_ref.shape[0]):
        for t in range(b_ref.shape[1]):
            line = jnp.where(lane == 8 + h * b_ref.shape[1] + t, b_ref[h, t], line)
    for n in range(c_ref.shape[0]):
        line = jnp.where(lane == 24 + n, c_ref[n], line)
    line_ref[...] = line
    copy.wait()


def line_of(a_where, b_where, c_where, blocks):
    smem = pl.BlockSpec(memory_space=pltpu.SMEM)
    vmem = pl.BlockSpec(memory_space=pltpu.VMEM)
    return pl.pallas_call(
        line_kernel,
        in_specs=[smem] * 3 + [pl.BlockSpec(memory_space=pl.ANY)],
        out_specs=[vmem, vmem],
        out_shape=[
            jax.ShapeDtypeStruct((1, 128), jnp.int32),
            jax.ShapeDtypeStruct(blocks.shape, blocks.dtype),
        ],
        scratch_shapes=[pltpu.SemaphoreType.DMA((1,))],
        compiler_params=pltpu.CompilerParams(vmem_limit_bytes=4 << 20),
        name="line",
    )(a_where, b_where, c_where, blocks)


def pair_kernel(tile_ref, beside_ref, _, pair_ref, __, sems):
    n = tile_ref.shape[0]
    copies = [
        pltpu.make_async_copy(tile_ref, pair_ref.at[pl.ds(0, n)], sems.at[0]),
        pltpu.make_async_copy(beside_ref, pair_ref.at[pl.ds(n, n)], sems.at[1]),
    ]
    for copy in copies:
        copy.start()
    for copy in copies:
        copy.wait()


def paired(tile, beside, passing):
    n, size = tile.shape[0], tile.shape[-1]
    anywhere = pl.BlockSpec(memory_space=pl.ANY)
    return pl.pallas_call(
        pair_kernel,
        in_specs=[anywhere] * 3,
        out_specs=[pl.BlockSpec(memory_space=pltpu.VMEM), anywhere],
        out_shape=[
            jax.ShapeDtypeStruct((2 * n, size, size), tile.dtype),
            jax.ShapeDtypeStruct(passing.shape, passing.dtype),
        ],
        scratch_shapes=[pltpu.SemaphoreType.DMA((2,))],
        input_output_aliases={2: 1},
        compiler_params=pltpu.CompilerParams(vmem_limit_bytes=4 << 20),
        name="pair",
    )(tile, beside, passing)


def hold_kernel(*refs):
    pass


def held_for(arrays, later):
    anywhere = pl.BlockSpec(memory_space=pl.ANY)
    return pl.pallas_call(
        hold_kernel,
        in_specs=[anywhere] * (len(arrays) + len(later)),
        out_specs=[anywhere] * len(arrays),
        out_shape=[jax.ShapeDtypeStruct(x.shape, x.dtype) for x in arrays],
        input_output_aliases={i: i for i in range(len(arrays))},
        compiler_params=pltpu.CompilerParams(vmem_limit_bytes=1 << 20),
        name="hold",
    )(*arrays, *later)


def among(held, bits, rows, columns):
    me = lax.axis_index("row") * columns + lax.axis_index(COL)
    group = jnp.zeros((2 ** len(bits),) + held.shape, held.dtype)
    for move in range(2 ** len(bits)):
        flip = sum(((move >> n) & 1) << bit for n, bit in enumerate(bits))
        got = held
        if move:
            pairs = [(i ^ flip, i) for i in range(rows * columns)]
            got = lax.ppermute(held, ("row", *COL), pairs)
        spot = sum((((me ^ flip) >> bit) & 1) << n for n, bit in enumerate(bits))
        group = lax.dynamic_update_index_in_dim(group, got, spot, 0)
    return group


def per_device(a_blocks, a_index, b_blocks, b_index, c_index):
    rows = lax.axis_size("row")
    columns = lax.axis_size(COL)
    row = lax.axis_index("row")
    me = jnp.stack([row, lax.axis_index(COL)])
    hold = columns // rows
    sa, sb, sc = a_blocks.shape[2], b_blocks.shape[3], c_index.shape[2]
    held = hold * sb
    size = a_blocks.shape[-1]

    own = b_blocks[0, 0].reshape(held, size, size)
    behind = to_row(own, rows, lambda i: (i + 2) % rows)
    ahead = to_row(own, rows, lambda i: (i - 2) % rows)
    near = [own, behind, ahead]

    mine, tile = line_of(a_index[0, 0], b_index[0, 0], c_index[0, 0], a_blocks[0, 0])
    spots = among(mine.reshape(128), (5, 6), rows, columns)
    pair, spots = paired(tile, moved(tile, lambda i: i ^ 8, columns), spots)
    spots = among(spots, (1, 2), rows, columns)
    spots = among(spots, (3, 4), rows, columns)
    spots = among(spots, (0,), rows, columns).reshape(rows * columns, 128)
    a_behind = moved(pair, on_z, columns)
    a_ahead = moved(pair, back_z, columns)

    sends = [
        (FAR, 3, lambda i: ((i + 2) & 7) ^ 1),
        (FAR, 2, lambda i: (i - 2) & 7),
        (NEAR, 1, lambda i: i ^ 1),
    ]
    pack_list, info, maps = plan(me, spots, sends)
    packed = pack(pack_list, near, [n for n, *_ in sends])

    far_other, far_own, cross = [
        to_row(block, rows, there) for block, (*_, there) in zip(packed, sends)
    ]

    over, product_list, zeros = overflow(me, info, spots, maps, sc, size)
    (a_behind,) = held_for([a_behind], [info])
    a_far = moved(a_behind, on_z, columns)
    (a_far,) = held_for([a_far], [far_other, far_own, cross, over])
    a_mine = [pair, a_behind, a_ahead, a_far]
    a_parts = a_mine + [moved(block, lambda i: i ^ 1, columns) for block in a_mine]

    b_parts = near + [cross, far_own, far_other]
    total = products(all_kernel, [product_list], a_parts, b_parts, zeros, sc)

    turns = over[0]

    def again(state):
        turn, total = state
        listing = relist(me, turn[None], info, sends)
        packed = pack(listing, near, [n for n, *_ in sends])
        far_other, far_own, cross = [
            to_row(block, rows, there) for block, (*_, there) in zip(packed, sends)
        ]
        blocks = [cross, far_own, far_other]
        leading = [me, turn[None], info]
        total = products(rest_kernel, leading, a_parts, blocks, total, sc, own_list=True)
        return turn + 1, total

    _, total = lax.while_loop(lambda state: state[0] <= turns, again, (jnp.int32(1), total))
    return total[None, None]


def solution(mesh):
    rows, columns = mesh.devices.shape
    mesh = Mesh(mesh.devices.reshape(rows, 2, columns // 4, 2), ("row", *COL))
    in_specs = (
        P("row", COL, None, None, None),
        P("row", COL, None),
        P("row", COL, None, None, None, None),
        P("row", COL, None, None),
        P("row", COL, None),
    )
    out_specs = P("row", COL, None, None, None)
    return jax.shard_map(
        per_device, mesh=mesh, in_specs=in_specs, out_specs=out_specs, check_vma=False
    )
```

profile of v0, /device:TPU:1, one launch (start us, length us, event | category | flops | bytes accessed | tf_op | source)
XLA Modules:
  0.0 62.7 jit_solution(1461295318316375859)
XLA Ops:
  0.0 0.0 copy-start.3
  0.0 0.0 copy-start.1
  0.0 0.6 %copy-done.3 = s32[1,1,16]{2,1,0:T(1,128)S(1)} copy-done((s32[1,1,16]{2,1,0:T(1,128)S(1)}, s32[1,1,16]{2,1,0:T(1,128)}, u32[]{:S(2)}) %copy-start.3) | copy-done | bytes 88
  0.7 0.0 copy-done.1
  0.7 0.0 copy-done.2
  0.7 0.0 copy-start
  0.7 0.9 %copy-done = f32[1,1,4,128,128]{4,3,2,1,0:T(8,128)S(1)} copy-done((f32[1,1,4,128,128]{4,3,2,1,0:T(8,128)S(1)}, f32[1,1,4,128,128]{4,3,2,1,0:T(8,128)}, u32[]{:S(2)}) %copy-start) | copy-done | bytes 262168
  1.6 0.6 line.1
  2.3 2.1 %collective-permute-start.3 = (f32[4,128,128]{2,1,0:T(8,128)S(1)}, f32[4,128,128]{2,1,0:T(8,128)S(1)}, u32[]{:S(2)}, u32[]{:S(2)}) collective-permute-start(f32[4,128,128]{2,1,0:T(8,128)S(1)} %get-tuple-element.104.tile_ref), channel_id=1, source_target_pairs={{0,8},{1,9},{2,10},{3,11},{4,12},{5,13},{6,14},{7,15},{8,0},{9,1},... | collective-permute-start | bytes 786440 | tf_op jit(solution)/shard_map/ppermute | solution.py:479
  4.4 1.3 %collective-permute-start.4 = (s32[128]{0:T(128)S(1)}, s32[128]{0:T(128)S(1)}, u32[]{:S(2)}, u32[]{:S(2)}) collective-permute-start(s32[128]{0:T(128)S(1)} %bitcast.43), channel_id=1, source_target_pairs={{32,0},{33,1},{34,2},{35,3},{36,4},{37,5},{38,6},{39,7},{40,8},{41... | collective-permute-start | bytes 1544 | tf_op jit(solution)/shard_map/ppermute | solution.py:570
  5.7 2.6 %collective-permute-start.5 = (s32[128]{0:T(128)S(1)}, s32[128]{0:T(128)S(1)}, u32[]{:S(2)}, u32[]{:S(2)}) collective-permute-start(s32[128]{0:T(128)S(1)} %bitcast.44), channel_id=1, source_target_pairs={{64,0},{65,1},{66,2},{67,3},{68,4},{69,5},{70,6},{71,7},{72,8},{73... | collective-permute-start | bytes 1544 | tf_op jit(solution)/shard_map/ppermute | solution.py:570
  8.3 0.0 collective-permute-start.6
  8.3 0.0 copy-start.4
  8.3 0.1 pad_add_fusion.me_ref
  8.4 0.0 collective-permute-start.17
  8.5 0.0 collective-permute-done.4
  8.5 2.7 %collective-permute-start.18 = (f32[16,128,128]{2,1,0:T(8,128)}, f32[16,128,128]{2,1,0:T(8,128)}, u32[]{:S(2)}, u32[]{:S(2)}) collective-permute-start(f32[16,128,128]{2,1,0:T(8,128)} %bitcast.47), channel_id=1, source_target_pairs={{0,96},{16,112},{32,0},{48,16},{64,32},{80,48},{96,64},{112,80},{1... | collective-permute-start | bytes 3145736 | tf_op jit(solution)/shard_map/ppermute | solution.py:467
  11.2 0.0 collective-permute-done.5
  11.3 0.6 %collective-permute-done.6 = s32[128]{0:T(128)S(1)} collective-permute-done((s32[128]{0:T(128)S(1)}, s32[128]{0:T(128)S(1)}, u32[]{:S(2)}, u32[]{:S(2)}) %collective-permute-start.6) | collective-permute-done | bytes 544 | tf_op jit(solution)/shard_map/ppermute | solution.py:570
  11.9 0.0 collective-permute-done.3.beside_ref
  11.9 0.1 pair.1
  12.0 1.7 %collective-permute-start.7 = (s32[4,128]{1,0:T(4,128)S(1)}, s32[4,128]{1,0:T(4,128)S(1)}, u32[]{:S(2)}, u32[]{:S(2)}) collective-permute-start(s32[4,128]{1,0:T(4,128)S(1)} %get-tuple-element.106), channel_id=1, source_target_pairs={{2,0},{3,1},{0,2},{1,3},{6,4},{7,5},{4,6},{5,7},{10,8},{11,9},{8,1... | collective-permute-start | bytes 6152 | tf_op jit(solution)/shard_map/ppermute | solution.py:570
  13.7 3.3 %collective-permute-start.8 = (s32[4,128]{1,0:T(4,128)S(1)}, s32[4,128]{1,0:T(4,128)S(1)}, u32[]{:S(2)}, u32[]{:S(2)}) collective-permute-start(s32[4,128]{1,0:T(4,128)S(1)} %get-tuple-element.106), channel_id=1, source_target_pairs={{4,0},{5,1},{6,2},{7,3},{0,4},{1,5},{2,6},{3,7},{12,8},{13,9},{14,... | collective-permute-start | bytes 6152 | tf_op jit(solution)/shard_map/ppermute | solution.py:570
  17.0 0.0 collective-permute-start.9
  17.0 0.0 collective-permute-done.7
  17.1 0.1 collective-permute-start.14
  17.2 0.9 %collective-permute-done.8 = s32[4,128]{1,0:T(4,128)S(1)} collective-permute-done((s32[4,128]{1,0:T(4,128)S(1)}, s32[4,128]{1,0:T(4,128)S(1)}, u32[]{:S(2)}, u32[]{:S(2)}) %collective-permute-start.8) | collective-permute-done | bytes 2080 | tf_op jit(solution)/shard_map/ppermute | solution.py:570
  18.0 3.1 %collective-permute-done.9 = s32[4,128]{1,0:T(4,128)S(1)} collective-permute-done((s32[4,128]{1,0:T(4,128)S(1)}, s32[4,128]{1,0:T(4,128)S(1)}, u32[]{:S(2)}, u32[]{:S(2)}) %collective-permute-start.9) | collective-permute-done | bytes 2080 | tf_op jit(solution)/shard_map/ppermute | solution.py:570
  21.1 0.3 collective-permute-start.10
  21.4 2.8 %collective-permute-start.11 = (s32[4,4,128]{2,1,0:T(4,128)S(1)}, s32[4,4,128]{2,1,0:T(4,128)S(1)}, u32[]{:S(2)}, u32[]{:S(2)}) collective-permute-start(s32[4,4,128]{2,1,0:T(4,128)S(1)} %constant_dynamic-update-slice_fusion), channel_id=1, source_target_pairs={{16,0},{17,1},{18,2},{19,3},{20,4},{21,5},{22,6},{23,7},{24,8},{25... | collective-permute-start | bytes 24584 | tf_op jit(solution)/shard_map/ppermute | solution.py:570
  24.2 0.0 collective-permute-done.10
  24.2 1.6 %collective-permute-start.12 = (s32[4,4,128]{2,1,0:T(4,128)S(1)}, s32[4,4,128]{2,1,0:T(4,128)S(1)}, u32[]{:S(2)}, u32[]{:S(2)}) collective-permute-start(s32[4,4,128]{2,1,0:T(4,128)S(1)} %constant_dynamic-update-slice_fusion), channel_id=1, source_target_pairs={{24,0},{25,1},{26,2},{27,3},{28,4},{29,5},{30,6},{31,7},{16,8},{17... | collective-permute-start | bytes 24584 | tf_op jit(solution)/shard_map/ppermute | solution.py:570
  25.8 0.0 collective-permute-done.11
  25.8 2.5 %collective-permute-done.12 = s32[4,4,128]{2,1,0:T(4,128)S(1)} collective-permute-done((s32[4,4,128]{2,1,0:T(4,128)S(1)}, s32[4,4,128]{2,1,0:T(4,128)S(1)}, u32[]{:S(2)}, u32[]{:S(2)}) %collective-permute-start.12) | collective-permute-done | bytes 8224 | tf_op jit(solution)/shard_map/ppermute | solution.py:570
  28.3 5.4 %collective-permute-start.13 = (s32[4,4,4,128]{3,2,1,0:T(4,128)S(1)}, s32[4,4,4,128]{3,2,1,0:T(4,128)S(1)}, u32[]{:S(2)}, u32[]{:S(2)}) collective-permute-start(s32[4,4,4,128]{3,2,1,0:T(4,128)S(1)} %bitcast_dynamic-update-slice_fusion.2), channel_id=1, source_target_pairs={{1,0},{0,1},{3,2},{2,3},{5,4},{4,5},{7,6},{6,7},{9,8},{8,9},{11,10... | collective-permute-start | bytes 98312 | tf_op jit(solution)/shard_map/ppermute | solution.py:570
  33.8 0.1 collective-permute-start.15
  33.9 0.7 %collective-permute-done.13 = s32[4,4,4,128]{3,2,1,0:T(4,128)S(1)} collective-permute-done((s32[4,4,4,128]{3,2,1,0:T(4,128)S(1)}, s32[4,4,4,128]{3,2,1,0:T(4,128)S(1)}, u32[]{:S(2)}, u32[]{:S(2)}) %collective-permute-start.13) | collective-permute-done | bytes 32800 | tf_op jit(solution)/shard_map/ppermute | solution.py:570
  34.6 1.8 %plan.1 = (s32[12]{0:T(128)S(1)}, s32[40,128]{1,0:T(8,128)S(1)}, bf16[6,128,128]{2,1,0:T(8,128)(2,1)S(1)}) custom-call(s32[2]{0:T(128)S(1)} %pad_add_fusion.me_ref, s32[128,128]{1,0:T(8,128)S(1)} %bitcast.38), custom_call_target="tpu_custom_call" | custom-call | tf_op jit(solution)/shard_map/plan/pallas_call | solution.py:178
  36.4 0.0 collective-permute-done.14.refs_0_
  36.5 0.8 %collective-permute-start.16 = (f32[8,128,128]{2,1,0:T(8,128)S(1)}, f32[8,128,128]{2,1,0:T(8,128)S(1)}, u32[]{:S(2)}, u32[]{:S(2)}) collective-permute-start(f32[8,128,128]{2,1,0:T(8,128)S(1)} %hold.2.rest_1_), channel_id=1, source_target_pairs={{0,2},{1,3},{2,4},{3,5},{4,6},{5,7},{6,0},{7,1},{8,10},{9,11},{10,... | collective-permute-start | bytes 1572872 | tf_op jit(solution)/shard_map/ppermute | solution.py:479
  37.2 0.0 collective-permute-done.17.rest_1_.rest_9_
  37.3 0.0 collective-permute-done.18.rest_2_.rest_10_
  37.3 0.0 copy-done.4
  37.3 0.8 %pack.2 = (f32[3,128,128]{2,1,0:T(8,128)S(1)}, f32[3,128,128]{2,1,0:T(8,128)S(1)}, f32[6,128,128]{2,1,0:T(8,128)S(1)}) custom-call(s32[12]{0:T(128)S(1)} %get-tuple-element.111.list_ref, f32[16,128,128]{2,1,0:T(8,128)S(1)} %bitcast.48, f32[16,128,128]{2,1,0:T(8,128)} %collective-permute-done.17.rest_1_.rest_9_, ...), custom_call_target="tpu_custom_call" | custom-call | tf_op jit(solution)/shard_map/pack/pallas_call | solution.py:211
  38.1 1.4 %collective-permute-start.21 = (f32[6,128,128]{2,1,0:T(8,128)S(1)}, f32[6,128,128]{2,1,0:T(8,128)S(1)}, u32[]{:S(2)}, u32[]{:S(2)}) collective-permute-start(f32[6,128,128]{2,1,0:T(8,128)S(1)} %get-tuple-element.114), channel_id=1, source_target_pairs={{0,16},{16,0},{32,48},{48,32},{64,80},{80,64},{96,112},{112,96},{1... | collective-permute-start | bytes 1179656 | tf_op jit(solution)/shard_map/ppermute | solution.py:467
  39.5 0.6 %collective-permute-start.19 = (f32[3,128,128]{2,1,0:T(8,128)S(1)}, f32[3,128,128]{2,1,0:T(8,128)S(1)}, u32[]{:S(2)}, u32[]{:S(2)}) collective-permute-start(f32[3,128,128]{2,1,0:T(8,128)S(1)} %get-tuple-element.112), channel_id=1, source_target_pairs={{0,48},{16,32},{32,80},{48,64},{64,112},{80,96},{96,16},{112,0},{1... | collective-permute-start | bytes 589832 | tf_op jit(solution)/shard_map/ppermute | solution.py:467
  40.1 3.4 %collective-permute-start.20 = (f32[3,128,128]{2,1,0:T(8,128)S(1)}, f32[3,128,128]{2,1,0:T(8,128)S(1)}, u32[]{:S(2)}, u32[]{:S(2)}) collective-permute-start(f32[3,128,128]{2,1,0:T(8,128)S(1)} %get-tuple-element.113), channel_id=1, source_target_pairs={{0,96},{16,112},{32,0},{48,16},{64,32},{80,48},{96,64},{112,80},{1... | collective-permute-start | bytes 589832 | tf_op jit(solution)/shard_map/ppermute | solution.py:467
  43.5 3.2 %overflow.1 = (s32[1]{0:T(128)}, s32[513]{0:T(1024)S(1)}, f32[16,128,128]{2,1,0:T(8,128)}) custom-call(s32[2]{0:T(128)S(1)} %pad_add_fusion.me_ref, s32[40,128]{1,0:T(8,128)S(1)} %get-tuple-element.258.info_ref.refs_1_, s32[128,128]{1,0:T(8,128)S(1)} %bitcast.39, bf16[6,128,128]{2,1,0:T(8,128)(2,1)S(1)} %get-tuple-element.108.maps_ref), custom_call_target="tpu_custom_call" | custom-call | flops 1000000000 | bytes 100000 | tf_op jit(solution)/shard_map/overflow/pallas_call | solution.py:258
  46.8 0.8 %collective-permute-done.15.rest_2_ = f32[8,128,128]{2,1,0:T(8,128)} collective-permute-done((f32[8,128,128]{2,1,0:T(8,128)S(1)}, f32[8,128,128]{2,1,0:T(8,128)}, u32[]{:S(2)}, u32[]{:S(2)}) %collective-permute-start.15) | collective-permute-done | bytes 524320 | tf_op jit(solution)/shard_map/ppermute | solution.py:479
  47.5 1.2 %collective-permute-start.22 = (f32[8,128,128]{2,1,0:T(8,128)S(1)}, f32[8,128,128]{2,1,0:T(8,128)}, u32[]{:S(2)}, u32[]{:S(2)}) collective-permute-start(f32[8,128,128]{2,1,0:T(8,128)S(1)} %get-tuple-element.262.rest_0_), channel_id=1, source_target_pairs={{0,1},{1,0},{2,3},{3,2},{4,5},{5,4},{6,7},{7,6},{8,9},{9,8},{10,11... | collective-permute-start | bytes 1572872 | tf_op jit(solution)/shard_map/ppermute | solution.py:479
  48.7 4.8 %collective-permute-done.19.refs_1_.rest_13_ = f32[3,128,128]{2,1,0:T(8,128)S(1)} collective-permute-done((f32[3,128,128]{2,1,0:T(8,128)S(1)}, f32[3,128,128]{2,1,0:T(8,128)S(1)}, u32[]{:S(2)}, u32[]{:S(2)}) %collective-permute-start.19) | collective-permute-done | bytes 196640 | tf_op jit(solution)/shard_map/ppermute | solution.py:467
  53.5 2.2 %collective-permute-start.23 = (f32[8,128,128]{2,1,0:T(8,128)S(1)}, f32[8,128,128]{2,1,0:T(8,128)}, u32[]{:S(2)}, u32[]{:S(2)}) collective-permute-start(f32[8,128,128]{2,1,0:T(8,128)S(1)} %hold.2.rest_1_), channel_id=1, source_target_pairs={{0,1},{1,0},{2,3},{3,2},{4,5},{5,4},{6,7},{7,6},{8,9},{9,8},{10,11... | collective-permute-start | bytes 1572872 | tf_op jit(solution)/shard_map/ppermute | solution.py:479
  55.7 0.0 collective-permute-done.20.refs_2_.rest_12_
  55.7 0.0 collective-permute-start.24
  55.7 0.0 collective-permute-done.16.refs_0_
  55.7 0.0 collective-permute-done.21.refs_3_.rest_11_
  55.8 0.6 %hold.3.rest_3_ = f32[8,128,128]{2,1,0:T(8,128)S(1)} custom-call(f32[8,128,128]{2,1,0:T(8,128)S(1)} %collective-permute-done.16.refs_0_, f32[3,128,128]{2,1,0:T(8,128)S(1)} %collective-permute-done.19.refs_1_.rest_13_, f32[3,128,128]{2,1,0:T(8,128)S(1)} %collective-permute-done.20.refs_2_.rest_12_, ...), custom_call_target="tpu_custom_call", output_to_operand_aliasing={{}: (0, {})} | custom-call | tf_op jit(solution)/shard_map/hold/pallas_call | solution.py:551
  56.4 0.6 collective-permute-start.25
  57.0 0.0 collective-permute-done.22.rest_4_
  57.0 1.1 %collective-permute-done.23.rest_5_ = f32[8,128,128]{2,1,0:T(8,128)} collective-permute-done((f32[8,128,128]{2,1,0:T(8,128)S(1)}, f32[8,128,128]{2,1,0:T(8,128)}, u32[]{:S(2)}, u32[]{:S(2)}) %collective-permute-start.23) | collective-permute-done | bytes 524320 | tf_op jit(solution)/shard_map/ppermute | solution.py:479
  58.1 0.4 collective-permute-done.24.rest_6_
  58.4 0.5 collective-permute-done.25.rest_7_
  58.9 3.2 %products.2 = f32[16,128,128]{2,1,0:T(8,128)} custom-call(s32[513]{0:T(1024)S(1)} %get-tuple-element.109.list_ref, f32[8,128,128]{2,1,0:T(8,128)S(1)} %get-tuple-element.262.rest_0_, f32[8,128,128]{2,1,0:T(8,128)S(1)} %hold.2.rest_1_, f32[8,128,128]{2,1,0:T(8,128)} %collective-permute-done.15.rest_2_, ...), custom_call_target="tpu_custom_call", output_to_operand_aliasing={{}: (15, {})} | custom-call | flops 100663296 | bytes 1572864 | tf_op jit(solution)/shard_map/products/pallas_call | solution.py:440
  62.1 0.6 %while.10 = (s32[]{:T(128)}, f32[16,128,128]{2,1,0:T(8,128)}, s32[]{:T(128)}, s32[2]{0:T(128)S(1)}, s32[40,128]{1,0:T(8,128)S(1)}, /*index=5*/f32[16,128,128]{2,...) while((s32[]{:T(128)}, f32[16,128,128]{2,1,0:T(8,128)}, ...), condition=%wide.region_1.2_spmd, body=%wide.region_0.1_spmd.sunk | while | flops 100663296 | bytes 13107597 | solution.py:636
  (20 shorter events, 0.2 us)
Async XLA Ops:
  0.0 0.7 %copy-start.3 = (s32[1,1,16]{2,1,0:T(1,128)S(1)}, s32[1,1,16]{2,1,0:T(1,128)}, u32[]{:S(2)}) copy-start(s32[1,1,16]{2,1,0:T(1,128)} %param.11) | copy-start | bytes 196
  0.0 0.7 %copy-start.1 = (s32[1,1,2,8]{3,2,1,0:T(2,128)S(1)}, s32[1,1,2,8]{3,2,1,0:T(2,128)}, u32[]{:S(2)}) copy-start(s32[1,1,2,8]{3,2,1,0:T(2,128)} %param.10) | copy-start | bytes 196
  0.0 0.7 %copy-start.2 = (s32[1,1,4]{2,1,0:T(1,128)S(1)}, s32[1,1,4]{2,1,0:T(1,128)}, u32[]{:S(2)}) copy-start(s32[1,1,4]{2,1,0:T(1,128)} %param.8) | copy-start | bytes 52
  0.7 1.0 %copy-start = (f32[1,1,4,128,128]{4,3,2,1,0:T(8,128)S(1)}, f32[1,1,4,128,128]{4,3,2,1,0:T(8,128)}, u32[]{:S(2)}) copy-start(f32[1,1,4,128,128]{4,3,2,1,0:T(8,128)} %param.7) | copy-start | bytes 786436
  2.3 9.7 %collective-permute-start.3 = (f32[4,128,128]{2,1,0:T(8,128)S(1)}, f32[4,128,128]{2,1,0:T(8,128)S(1)}, u32[]{:S(2)}, u32[]{:S(2)}) collective-permute-start(f32[4,128,128]{2,1,0:T(8,128)S(1)} %get-tuple-element.104.tile_ref), channel_id=1, source_target_pairs={{0,8},{1,9},{2,10},{3,11},{4,12},{5,13},{6,14},{7,15},{8,0},{9,1},... | collective-permute-start | bytes 786440 | tf_op jit(solution)/shard_map/ppermute | solution.py:479
  4.4 4.1 %collective-permute-start.4 = (s32[128]{0:T(128)S(1)}, s32[128]{0:T(128)S(1)}, u32[]{:S(2)}, u32[]{:S(2)}) collective-permute-start(s32[128]{0:T(128)S(1)} %bitcast.43), channel_id=1, source_target_pairs={{32,0},{33,1},{34,2},{35,3},{36,4},{37,5},{38,6},{39,7},{40,8},{41... | collective-permute-start | bytes 1544 | tf_op jit(solution)/shard_map/ppermute | solution.py:570
  5.7 5.5 %collective-permute-start.5 = (s32[128]{0:T(128)S(1)}, s32[128]{0:T(128)S(1)}, u32[]{:S(2)}, u32[]{:S(2)}) collective-permute-start(s32[128]{0:T(128)S(1)} %bitcast.44), channel_id=1, source_target_pairs={{64,0},{65,1},{66,2},{67,3},{68,4},{69,5},{70,6},{71,7},{72,8},{73... | collective-permute-start | bytes 1544 | tf_op jit(solution)/shard_map/ppermute | solution.py:570
  8.3 3.6 %collective-permute-start.6 = (s32[128]{0:T(128)S(1)}, s32[128]{0:T(128)S(1)}, u32[]{:S(2)}, u32[]{:S(2)}) collective-permute-start(s32[128]{0:T(128)S(1)} %bitcast.45), channel_id=1, source_target_pairs={{96,0},{97,1},{98,2},{99,3},{100,4},{101,5},{102,6},{103,7},{104,8... | collective-permute-start | bytes 1544 | tf_op jit(solution)/shard_map/ppermute | solution.py:570
  8.3 28.9 %copy-start.4 = (f32[1,1,2,8,128,128]{5,4,3,2,1,0:T(8,128)S(1)}, f32[1,1,2,8,128,128]{5,4,3,2,1,0:T(8,128)}, u32[]{:S(2)}) copy-start(f32[1,1,2,8,128,128]{5,4,3,2,1,0:T(8,128)} %param.9) | copy-start | bytes 3145732
  8.4 28.8 %collective-permute-start.17 = (f32[16,128,128]{2,1,0:T(8,128)}, f32[16,128,128]{2,1,0:T(8,128)}, u32[]{:S(2)}, u32[]{:S(2)}) collective-permute-start(f32[16,128,128]{2,1,0:T(8,128)} %bitcast.46), channel_id=1, source_target_pairs={{0,32},{16,48},{32,64},{48,80},{64,96},{80,112},{96,0},{112,16},{1... | collective-permute-start | bytes 3145736 | tf_op jit(solution)/shard_map/ppermute | solution.py:467
  8.5 28.8 %collective-permute-start.18 = (f32[16,128,128]{2,1,0:T(8,128)}, f32[16,128,128]{2,1,0:T(8,128)}, u32[]{:S(2)}, u32[]{:S(2)}) collective-permute-start(f32[16,128,128]{2,1,0:T(8,128)} %bitcast.47), channel_id=1, source_target_pairs={{0,96},{16,112},{32,0},{48,16},{64,32},{80,48},{96,64},{112,80},{1... | collective-permute-start | bytes 3145736 | tf_op jit(solution)/shard_map/ppermute | solution.py:467
  12.0 5.0 %collective-permute-start.7 = (s32[4,128]{1,0:T(4,128)S(1)}, s32[4,128]{1,0:T(4,128)S(1)}, u32[]{:S(2)}, u32[]{:S(2)}) collective-permute-start(s32[4,128]{1,0:T(4,128)S(1)} %get-tuple-element.106), channel_id=1, source_target_pairs={{2,0},{3,1},{0,2},{1,3},{6,4},{7,5},{4,6},{5,7},{10,8},{11,9},{8,1... | collective-permute-start | bytes 6152 | tf_op jit(solution)/shard_map/ppermute | solution.py:570
  13.7 4.3 %collective-permute-start.8 = (s32[4,128]{1,0:T(4,128)S(1)}, s32[4,128]{1,0:T(4,128)S(1)}, u32[]{:S(2)}, u32[]{:S(2)}) collective-permute-start(s32[4,128]{1,0:T(4,128)S(1)} %get-tuple-element.106), channel_id=1, source_target_pairs={{4,0},{5,1},{6,2},{7,3},{0,4},{1,5},{2,6},{3,7},{12,8},{13,9},{14,... | collective-permute-start | bytes 6152 | tf_op jit(solution)/shard_map/ppermute | solution.py:570
  17.0 4.0 %collective-permute-start.9 = (s32[4,128]{1,0:T(4,128)S(1)}, s32[4,128]{1,0:T(4,128)S(1)}, u32[]{:S(2)}, u32[]{:S(2)}) collective-permute-start(s32[4,128]{1,0:T(4,128)S(1)} %get-tuple-element.106), channel_id=1, source_target_pairs={{6,0},{7,1},{4,2},{5,3},{2,4},{3,5},{0,6},{1,7},{14,8},{15,9},{12,... | collective-permute-start | bytes 6152 | tf_op jit(solution)/shard_map/ppermute | solution.py:570
  17.1 19.4 %collective-permute-start.14 = (f32[8,128,128]{2,1,0:T(8,128)S(1)}, f32[8,128,128]{2,1,0:T(8,128)S(1)}, u32[]{:S(2)}, u32[]{:S(2)}) collective-permute-start(f32[8,128,128]{2,1,0:T(8,128)S(1)} %get-tuple-element.262.rest_0_), channel_id=1, source_target_pairs={{0,2},{1,3},{2,4},{3,5},{4,6},{5,7},{6,0},{7,1},{8,10},{9,11},{10,... | collective-permute-start | bytes 1572872 | tf_op jit(solution)/shard_map/ppermute | solution.py:479
  21.1 3.1 %collective-permute-start.10 = (s32[4,4,128]{2,1,0:T(4,128)S(1)}, s32[4,4,128]{2,1,0:T(4,128)S(1)}, u32[]{:S(2)}, u32[]{:S(2)}) collective-permute-start(s32[4,4,128]{2,1,0:T(4,128)S(1)} %constant_dynamic-update-slice_fusion), channel_id=1, source_target_pairs={{8,0},{9,1},{10,2},{11,3},{12,4},{13,5},{14,6},{15,7},{0,8},{1,9},... | collective-permute-start | bytes 24584 | tf_op jit(solution)/shard_map/ppermute | solution.py:570
  21.4 4.5 %collective-permute-start.11 = (s32[4,4,128]{2,1,0:T(4,128)S(1)}, s32[4,4,128]{2,1,0:T(4,128)S(1)}, u32[]{:S(2)}, u32[]{:S(2)}) collective-permute-start(s32[4,4,128]{2,1,0:T(4,128)S(1)} %constant_dynamic-update-slice_fusion), channel_id=1, source_target_pairs={{16,0},{17,1},{18,2},{19,3},{20,4},{21,5},{22,6},{23,7},{24,8},{25... | collective-permute-start | bytes 24584 | tf_op jit(solution)/shard_map/ppermute | solution.py:570
  24.2 4.1 %collective-permute-start.12 = (s32[4,4,128]{2,1,0:T(4,128)S(1)}, s32[4,4,128]{2,1,0:T(4,128)S(1)}, u32[]{:S(2)}, u32[]{:S(2)}) collective-permute-start(s32[4,4,128]{2,1,0:T(4,128)S(1)} %constant_dynamic-update-slice_fusion), channel_id=1, source_target_pairs={{24,0},{25,1},{26,2},{27,3},{28,4},{29,5},{30,6},{31,7},{16,8},{17... | collective-permute-start | bytes 24584 | tf_op jit(solution)/shard_map/ppermute | solution.py:570
  28.3 6.3 %collective-permute-start.13 = (s32[4,4,4,128]{3,2,1,0:T(4,128)S(1)}, s32[4,4,4,128]{3,2,1,0:T(4,128)S(1)}, u32[]{:S(2)}, u32[]{:S(2)}) collective-permute-start(s32[4,4,4,128]{3,2,1,0:T(4,128)S(1)} %bitcast_dynamic-update-slice_fusion.2), channel_id=1, source_target_pairs={{1,0},{0,1},{3,2},{2,3},{5,4},{4,5},{7,6},{6,7},{9,8},{8,9},{11,10... | collective-permute-start | bytes 98312 | tf_op jit(solution)/shard_map/ppermute | solution.py:570
  33.8 13.7 %collective-permute-start.15 = (f32[8,128,128]{2,1,0:T(8,128)S(1)}, f32[8,128,128]{2,1,0:T(8,128)}, u32[]{:S(2)}, u32[]{:S(2)}) collective-permute-start(f32[8,128,128]{2,1,0:T(8,128)S(1)} %get-tuple-element.262.rest_0_), channel_id=1, source_target_pairs={{0,6},{1,7},{2,0},{3,1},{4,2},{5,3},{6,4},{7,5},{8,14},{9,15},{10,... | collective-permute-start | bytes 1572872 | tf_op jit(solution)/shard_map/ppermute | solution.py:479
  36.5 19.3 %collective-permute-start.16 = (f32[8,128,128]{2,1,0:T(8,128)S(1)}, f32[8,128,128]{2,1,0:T(8,128)S(1)}, u32[]{:S(2)}, u32[]{:S(2)}) collective-permute-start(f32[8,128,128]{2,1,0:T(8,128)S(1)} %hold.2.rest_1_), channel_id=1, source_target_pairs={{0,2},{1,3},{2,4},{3,5},{4,6},{5,7},{6,0},{7,1},{8,10},{9,11},{10,... | collective-permute-start | bytes 1572872 | tf_op jit(solution)/shard_map/ppermute | solution.py:479
  38.1 17.7 %collective-permute-start.21 = (f32[6,128,128]{2,1,0:T(8,128)S(1)}, f32[6,128,128]{2,1,0:T(8,128)S(1)}, u32[]{:S(2)}, u32[]{:S(2)}) collective-permute-start(f32[6,128,128]{2,1,0:T(8,128)S(1)} %get-tuple-element.114), channel_id=1, source_target_pairs={{0,16},{16,0},{32,48},{48,32},{64,80},{80,64},{96,112},{112,96},{1... | collective-permute-start | bytes 1179656 | tf_op jit(solution)/shard_map/ppermute | solution.py:467
  39.5 14.0 %collective-permute-start.19 = (f32[3,128,128]{2,1,0:T(8,128)S(1)}, f32[3,128,128]{2,1,0:T(8,128)S(1)}, u32[]{:S(2)}, u32[]{:S(2)}) collective-permute-start(f32[3,128,128]{2,1,0:T(8,128)S(1)} %get-tuple-element.112), channel_id=1, source_target_pairs={{0,48},{16,32},{32,80},{48,64},{64,112},{80,96},{96,16},{112,0},{1... | collective-permute-start | bytes 589832 | tf_op jit(solution)/shard_map/ppermute | solution.py:467
  40.1 15.6 %collective-permute-start.20 = (f32[3,128,128]{2,1,0:T(8,128)S(1)}, f32[3,128,128]{2,1,0:T(8,128)S(1)}, u32[]{:S(2)}, u32[]{:S(2)}) collective-permute-start(f32[3,128,128]{2,1,0:T(8,128)S(1)} %get-tuple-element.113), channel_id=1, source_target_pairs={{0,96},{16,112},{32,0},{48,16},{64,32},{80,48},{96,64},{112,80},{1... | collective-permute-start | bytes 589832 | tf_op jit(solution)/shard_map/ppermute | solution.py:467
  47.5 9.5 %collective-permute-start.22 = (f32[8,128,128]{2,1,0:T(8,128)S(1)}, f32[8,128,128]{2,1,0:T(8,128)}, u32[]{:S(2)}, u32[]{:S(2)}) collective-permute-start(f32[8,128,128]{2,1,0:T(8,128)S(1)} %get-tuple-element.262.rest_0_), channel_id=1, source_target_pairs={{0,1},{1,0},{2,3},{3,2},{4,5},{5,4},{6,7},{7,6},{8,9},{9,8},{10,11... | collective-permute-start | bytes 1572872 | tf_op jit(solution)/shard_map/ppermute | solution.py:479
  53.5 4.6 %collective-permute-start.23 = (f32[8,128,128]{2,1,0:T(8,128)S(1)}, f32[8,128,128]{2,1,0:T(8,128)}, u32[]{:S(2)}, u32[]{:S(2)}) collective-permute-start(f32[8,128,128]{2,1,0:T(8,128)S(1)} %hold.2.rest_1_), channel_id=1, source_target_pairs={{0,1},{1,0},{2,3},{3,2},{4,5},{5,4},{6,7},{7,6},{8,9},{9,8},{10,11... | collective-permute-start | bytes 1572872 | tf_op jit(solution)/shard_map/ppermute | solution.py:479
  55.7 2.7 %collective-permute-start.24 = (f32[8,128,128]{2,1,0:T(8,128)}, f32[8,128,128]{2,1,0:T(8,128)}, u32[]{:S(2)}, u32[]{:S(2)}) collective-permute-start(f32[8,128,128]{2,1,0:T(8,128)} %collective-permute-done.15.rest_2_), channel_id=1, source_target_pairs={{0,1},{1,0},{2,3},{3,2},{4,5},{5,4},{6,7},{7,6},{8,9},{9,8},{10,11... | collective-permute-start | bytes 1572872 | tf_op jit(solution)/shard_map/ppermute | solution.py:479
  56.4 2.5 %collective-permute-start.25 = (f32[8,128,128]{2,1,0:T(8,128)S(1)}, f32[8,128,128]{2,1,0:T(8,128)}, u32[]{:S(2)}, u32[]{:S(2)}) collective-permute-start(f32[8,128,128]{2,1,0:T(8,128)S(1)} %hold.3.rest_3_), channel_id=1, source_target_pairs={{0,1},{1,0},{2,3},{3,2},{4,5},{5,4},{6,7},{7,6},{8,9},{9,8},{10,11... | collective-permute-start | bytes 1572872 | tf_op jit(solution)/shard_map/ppermute | solution.py:479
where the time goes:
time: 63.1 us; the launch traced here: 62.7 us
  starting transfers between devices  34.3 us (54%)
  waiting for transfers between devices  15.3 us (24%)
  Pallas kernels  10.3 us (16%)
  local copies, waits for them, and re-layouts  1.89 us (3%)
  loops' own time  0.64 us (1%)
    ppermute x10, starting transfers between devices, among(): got = lax.ppermute(held, ('row', *COL), pairs)  19.1 us
    ppermute x5, starting transfers between devices, to_row(): return lax.ppermute(block, 'row', [(i, there(i)) for i in range(rows)])  8.2 us
    ppermute x10, waiting for transfers between devices, among(): got = lax.ppermute(held, ('row', *COL), pairs)  7.81 us
    ppermute x8, starting transfers between devices, moved(): return lax.ppermute(block, COL, [(i, there(i)) for i in range(columns)])  7.05 us
    ppermute x5, waiting for transfers between devices, to_row(): return lax.ppermute(block, 'row', [(i, there(i)) for i in range(rows)])  4.81 us
    pallas_call x1, Pallas kernels, overflow(): pl.pallas_call(overflow_kernel, in_specs=[smem, vmem, vmem, vmem], out_sp...  3.23 us
    pallas_call x1, Pallas kernels, products(): pl.pallas_call(functools.partial(kernel, parts), in_specs=[smem if x.ndim...  3.18 us
    ppermute x8, waiting for transfers between devices, moved(): return lax.ppermute(block, COL, [(i, there(i)) for i in range(columns)])  2.7 us
  transfers between devices with their start and end apart: 23, of which 10 were waited for; matrix products, arithmetic and copies ran while one was open for 1% of the time, Pallas kernels for 10%

commit v1 on v0

--- a/solution.py
+++ b/solution.py
@@ -479,9 +479,17 @@
     return lax.ppermute(block, COL, [(i, there(i)) for i in range(columns)])
 
 
-def line_kernel(a_ref, b_ref, c_ref, blocks_ref, line_ref, tile_ref, sem):
-    copy = pltpu.make_async_copy(blocks_ref, tile_ref, sem.at[0])
-    copy.start()
+def line_kernel(a_in, b_in, c_in, blocks_ref, line_ref, tile_ref, a_ref, b_ref, c_ref, sem):
+    copies = [
+        pltpu.make_async_copy(source, target, sem.at[n])
+        for n, (source, target) in enumerate(
+            [(a_in, a_ref), (b_in, b_ref), (c_in, c_ref), (blocks_ref, tile_ref)]
+        )
+    ]
+    for copy in copies:
+        copy.start()
+    for copy in copies[:3]:
+        copy.wait()
     lane = lax.broadcasted_iota(jnp.int32, line_ref.shape, 1)
     line = jnp.full(line_ref.shape, -1, jnp.int32)
     for n in range(a_ref.shape[0]):
@@ -492,21 +500,22 @@
     for n in range(c_ref.shape[0]):
         line = jnp.where(lane == 24 + n, c_ref[n], line)
     line_ref[...] = line
-    copy.wait()
+    copies[3].wait()
 
 
 def line_of(a_where, b_where, c_where, blocks):
-    smem = pl.BlockSpec(memory_space=pltpu.SMEM)
+    anywhere = pl.BlockSpec(memory_space=pl.ANY)
     vmem = pl.BlockSpec(memory_space=pltpu.VMEM)
     return pl.pallas_call(
         line_kernel,
-        in_specs=[smem] * 3 + [pl.BlockSpec(memory_space=pl.ANY)],
+        in_specs=[anywhere] * 4,
         out_specs=[vmem, vmem],
         out_shape=[
             jax.ShapeDtypeStruct((1, 128), jnp.int32),
             jax.ShapeDtypeStruct(blocks.shape, blocks.dtype),
         ],
-        scratch_shapes=[pltpu.SemaphoreType.DMA((1,))],
+        scratch_shapes=[pltpu.SMEM(x.shape, x.dtype) for x in (a_where, b_where, c_where)]
+        + [pltpu.SemaphoreType.DMA((4,))],
         compiler_params=pltpu.CompilerParams(vmem_limit_bytes=4 << 20),
         name="line",
     )(a_where, b_where, c_where, blocks)

time: 63.1 us -> 63.5 us (level)
    ppermute x5, waiting for transfers between devices: 4.81 us -> 6.02 us  [to_row(): return lax.ppermute(block, 'row', [(i, there(i)) for i in range(rows)])]
    pallas_call x1, Pallas kernels: 0.8 us -> 1.5 us  [pack(): pl.pallas_call(functools.partial(pack_kernel, sizes), in_specs=[pl.BlockS...]
  transfers between devices with their start and end apart: 23 -> 23, of which waited for: 10 -> 10; matrix products, arithmetic and copies ran while one was open for 1% -> 1% of each run, Pallas kernels for 10% -> 11%
where the time goes in v1:
time: 63.5 us; the launch traced here: 63.2 us
  starting transfers between devices  33.9 us (53%)
  waiting for transfers between devices  15.9 us (25%)
  Pallas kernels  10.7 us (17%)
  local copies, waits for them, and re-layouts  1.89 us (3%)
  loops' own time  0.64 us (1%)
    ppermute x10, starting transfers between devices, among(): got = lax.ppermute(held, ('row', *COL), pairs)  19.1 us
    ppermute x5, starting transfers between devices, to_row(): return lax.ppermute(block, 'row', [(i, there(i)) for i in range(rows)])  8.2 us
    ppermute x10, waiting for transfers between devices, among(): got = lax.ppermute(held, ('row', *COL), pairs)  7.81 us
    ppermute x8, starting transfers between devices, moved(): return lax.ppermute(block, COL, [(i, there(i)) for i in range(columns)])  6.58 us
    ppermute x5, waiting for transfers between devices, to_row(): return lax.ppermute(block, 'row', [(i, there(i)) for i in range(rows)])  6.02 us
    pallas_call x1, Pallas kernels, overflow(): pl.pallas_call(overflow_kernel, in_specs=[smem, vmem, vmem, vmem], out_sp...  3.11 us
    pallas_call x1, Pallas kernels, products(): pl.pallas_call(functools.partial(kernel, parts), in_specs=[smem if x.ndim...  2.93 us
    ppermute x8, waiting for transfers between devices, moved(): return lax.ppermute(block, COL, [(i, there(i)) for i in range(columns)])  2.12 us
  transfers between devices with their start and end apart: 23, of which 10 were waited for; matrix products, arithmetic and copies ran while one was open for 1% of the time, Pallas kernels for 11%

profile of v1, /device:TPU:1, one launch (start us, length us, event | category | flops | bytes accessed | tf_op | source)
XLA Modules:
  0.0 63.2 jit_solution(17408078946198173123)
XLA Ops:
  0.0 0.0 copy-start.3
  0.0 0.0 copy-start.1
  0.0 0.0 copy-start.2
  0.0 0.6 %copy-done.3 = s32[1,1,16]{2,1,0:T(1,128)S(1)} copy-done((s32[1,1,16]{2,1,0:T(1,128)S(1)}, s32[1,1,16]{2,1,0:T(1,128)}, u32[]{:S(2)}) %copy-start.3) | copy-done | bytes 88
  0.7 0.0 copy-done.1
  0.7 0.0 copy-done.2
  0.7 0.0 copy-start
  0.7 0.9 %copy-done = f32[1,1,4,128,128]{4,3,2,1,0:T(8,128)S(1)} copy-done((f32[1,1,4,128,128]{4,3,2,1,0:T(8,128)S(1)}, f32[1,1,4,128,128]{4,3,2,1,0:T(8,128)}, u32[]{:S(2)}) %copy-start) | copy-done | bytes 262168
  1.6 0.6 line.1
  2.3 2.1 %collective-permute-start.3 = (f32[4,128,128]{2,1,0:T(8,128)S(1)}, f32[4,128,128]{2,1,0:T(8,128)S(1)}, u32[]{:S(2)}, u32[]{:S(2)}) collective-permute-start(f32[4,128,128]{2,1,0:T(8,128)S(1)} %get-tuple-element.104.tile_ref), channel_id=1, source_target_pairs={{0,8},{1,9},{2,10},{3,11},{4,12},{5,13},{6,14},{7,15},{8,0},{9,1},... | collective-permute-start | bytes 786440 | tf_op jit(solution)/shard_map/ppermute | solution.py:479
  4.4 1.3 %collective-permute-start.4 = (s32[128]{0:T(128)S(1)}, s32[128]{0:T(128)S(1)}, u32[]{:S(2)}, u32[]{:S(2)}) collective-permute-start(s32[128]{0:T(128)S(1)} %bitcast.43), channel_id=1, source_target_pairs={{32,0},{33,1},{34,2},{35,3},{36,4},{37,5},{38,6},{39,7},{40,8},{41... | collective-permute-start | bytes 1544 | tf_op jit(solution)/shard_map/ppermute | solution.py:579
  5.7 2.6 %collective-permute-start.5 = (s32[128]{0:T(128)S(1)}, s32[128]{0:T(128)S(1)}, u32[]{:S(2)}, u32[]{:S(2)}) collective-permute-start(s32[128]{0:T(128)S(1)} %bitcast.44), channel_id=1, source_target_pairs={{64,0},{65,1},{66,2},{67,3},{68,4},{69,5},{70,6},{71,7},{72,8},{73... | collective-permute-start | bytes 1544 | tf_op jit(solution)/shard_map/ppermute | solution.py:579
  8.3 0.0 collective-permute-start.6
  8.4 0.1 pad_add_fusion.me_ref
  8.4 0.0 collective-permute-start.17
  8.5 0.0 collective-permute-done.4
  8.5 2.7 %collective-permute-start.18 = (f32[16,128,128]{2,1,0:T(8,128)}, f32[16,128,128]{2,1,0:T(8,128)}, u32[]{:S(2)}, u32[]{:S(2)}) collective-permute-start(f32[16,128,128]{2,1,0:T(8,128)} %bitcast.47), channel_id=1, source_target_pairs={{0,96},{16,112},{32,0},{48,16},{64,32},{80,48},{96,64},{112,80},{1... | collective-permute-start | bytes 3145736 | tf_op jit(solution)/shard_map/ppermute | solution.py:467
  11.2 0.0 collective-permute-done.5
  11.3 0.6 %collective-permute-done.6 = s32[128]{0:T(128)S(1)} collective-permute-done((s32[128]{0:T(128)S(1)}, s32[128]{0:T(128)S(1)}, u32[]{:S(2)}, u32[]{:S(2)}) %collective-permute-start.6) | collective-permute-done | bytes 544 | tf_op jit(solution)/shard_map/ppermute | solution.py:579
  11.9 0.0 collective-permute-done.3.beside_ref
  12.0 0.1 pair.1
  12.0 1.7 %collective-permute-start.7 = (s32[4,128]{1,0:T(4,128)S(1)}, s32[4,128]{1,0:T(4,128)S(1)}, u32[]{:S(2)}, u32[]{:S(2)}) collective-permute-start(s32[4,128]{1,0:T(4,128)S(1)} %get-tuple-element.106), channel_id=1, source_target_pairs={{2,0},{3,1},{0,2},{1,3},{6,4},{7,5},{4,6},{5,7},{10,8},{11,9},{8,1... | collective-permute-start | bytes 6152 | tf_op jit(solution)/shard_map/ppermute | solution.py:579
  13.7 3.3 %collective-permute-start.8 = (s32[4,128]{1,0:T(4,128)S(1)}, s32[4,128]{1,0:T(4,128)S(1)}, u32[]{:S(2)}, u32[]{:S(2)}) collective-permute-start(s32[4,128]{1,0:T(4,128)S(1)} %get-tuple-element.106), channel_id=1, source_target_pairs={{4,0},{5,1},{6,2},{7,3},{0,4},{1,5},{2,6},{3,7},{12,8},{13,9},{14,... | collective-permute-start | bytes 6152 | tf_op jit(solution)/shard_map/ppermute | solution.py:579
  17.0 0.0 collective-permute-start.9
  17.1 0.0 collective-permute-done.7
  17.1 0.1 collective-permute-start.14
  17.2 0.9 %collective-permute-done.8 = s32[4,128]{1,0:T(4,128)S(1)} collective-permute-done((s32[4,128]{1,0:T(4,128)S(1)}, s32[4,128]{1,0:T(4,128)S(1)}, u32[]{:S(2)}, u32[]{:S(2)}) %collective-permute-start.8) | collective-permute-done | bytes 2080 | tf_op jit(solution)/shard_map/ppermute | solution.py:579
  18.0 3.1 %collective-permute-done.9 = s32[4,128]{1,0:T(4,128)S(1)} collective-permute-done((s32[4,128]{1,0:T(4,128)S(1)}, s32[4,128]{1,0:T(4,128)S(1)}, u32[]{:S(2)}, u32[]{:S(2)}) %collective-permute-start.9) | collective-permute-done | bytes 2080 | tf_op jit(solution)/shard_map/ppermute | solution.py:579
  21.1 0.3 collective-permute-start.10
  21.4 2.8 %collective-permute-start.11 = (s32[4,4,128]{2,1,0:T(4,128)S(1)}, s32[4,4,128]{2,1,0:T(4,128)S(1)}, u32[]{:S(2)}, u32[]{:S(2)}) collective-permute-start(s32[4,4,128]{2,1,0:T(4,128)S(1)} %constant_dynamic-update-slice_fusion), channel_id=1, source_target_pairs={{16,0},{17,1},{18,2},{19,3},{20,4},{21,5},{22,6},{23,7},{24,8},{25... | collective-permute-start | bytes 24584 | tf_op jit(solution)/shard_map/ppermute | solution.py:579
  24.2 0.0 collective-permute-done.10
  24.2 1.6 %collective-permute-start.12 = (s32[4,4,128]{2,1,0:T(4,128)S(1)}, s32[4,4,128]{2,1,0:T(4,128)S(1)}, u32[]{:S(2)}, u32[]{:S(2)}) collective-permute-start(s32[4,4,128]{2,1,0:T(4,128)S(1)} %constant_dynamic-update-slice_fusion), channel_id=1, source_target_pairs={{24,0},{25,1},{26,2},{27,3},{28,4},{29,5},{30,6},{31,7},{16,8},{17... | collective-permute-start | bytes 24584 | tf_op jit(solution)/shard_map/ppermute | solution.py:579
  25.8 0.0 collective-permute-done.11
  25.8 2.5 %collective-permute-done.12 = s32[4,4,128]{2,1,0:T(4,128)S(1)} collective-permute-done((s32[4,4,128]{2,1,0:T(4,128)S(1)}, s32[4,4,128]{2,1,0:T(4,128)S(1)}, u32[]{:S(2)}, u32[]{:S(2)}) %collective-permute-start.12) | collective-permute-done | bytes 8224 | tf_op jit(solution)/shard_map/ppermute | solution.py:579
  28.3 5.4 %collective-permute-start.13 = (s32[4,4,4,128]{3,2,1,0:T(4,128)S(1)}, s32[4,4,4,128]{3,2,1,0:T(4,128)S(1)}, u32[]{:S(2)}, u32[]{:S(2)}) collective-permute-start(s32[4,4,4,128]{3,2,1,0:T(4,128)S(1)} %bitcast_dynamic-update-slice_fusion.2), channel_id=1, source_target_pairs={{1,0},{0,1},{3,2},{2,3},{5,4},{4,5},{7,6},{6,7},{9,8},{8,9},{11,10... | collective-permute-start | bytes 98312 | tf_op jit(solution)/shard_map/ppermute | solution.py:579
  33.8 0.1 collective-permute-start.15
  33.9 0.7 %collective-permute-done.13 = s32[4,4,4,128]{3,2,1,0:T(4,128)S(1)} collective-permute-done((s32[4,4,4,128]{3,2,1,0:T(4,128)S(1)}, s32[4,4,4,128]{3,2,1,0:T(4,128)S(1)}, u32[]{:S(2)}, u32[]{:S(2)}) %collective-permute-start.13) | collective-permute-done | bytes 32800 | tf_op jit(solution)/shard_map/ppermute | solution.py:579
  34.6 1.8 %plan.1 = (s32[12]{0:T(128)S(1)}, s32[40,128]{1,0:T(8,128)S(1)}, bf16[6,128,128]{2,1,0:T(8,128)(2,1)S(1)}) custom-call(s32[2]{0:T(128)S(1)} %pad_add_fusion.me_ref, s32[128,128]{1,0:T(8,128)S(1)} %bitcast.38), custom_call_target="tpu_custom_call" | custom-call | tf_op jit(solution)/shard_map/plan/pallas_call | solution.py:178
  36.5 0.0 collective-permute-done.14.refs_0_
  36.5 0.8 %collective-permute-start.16 = (f32[8,128,128]{2,1,0:T(8,128)S(1)}, f32[8,128,128]{2,1,0:T(8,128)S(1)}, u32[]{:S(2)}, u32[]{:S(2)}) collective-permute-start(f32[8,128,128]{2,1,0:T(8,128)S(1)} %hold.2.rest_1_), channel_id=1, source_target_pairs={{0,2},{1,3},{2,4},{3,5},{4,6},{5,7},{6,0},{7,1},{8,10},{9,11},{10,... | collective-permute-start | bytes 1572872 | tf_op jit(solution)/shard_map/ppermute | solution.py:479
  37.3 0.0 collective-permute-done.17.rest_1_.rest_9_
  37.3 0.0 collective-permute-done.18.rest_2_.rest_10_
  37.3 0.0 copy-done.4
  37.3 1.5 %pack.2 = (f32[3,128,128]{2,1,0:T(8,128)S(1)}, f32[3,128,128]{2,1,0:T(8,128)S(1)}, f32[6,128,128]{2,1,0:T(8,128)S(1)}) custom-call(s32[12]{0:T(128)S(1)} %get-tuple-element.111.list_ref, f32[16,128,128]{2,1,0:T(8,128)S(1)} %bitcast.48, f32[16,128,128]{2,1,0:T(8,128)} %collective-permute-done.17.rest_1_.rest_9_, ...), custom_call_target="tpu_custom_call" | custom-call | tf_op jit(solution)/shard_map/pack/pallas_call | solution.py:211
  38.8 0.6 collective-permute-start.21
  39.4 0.6 collective-permute-start.19
  40.0 4.2 %collective-permute-start.20 = (f32[3,128,128]{2,1,0:T(8,128)S(1)}, f32[3,128,128]{2,1,0:T(8,128)S(1)}, u32[]{:S(2)}, u32[]{:S(2)}) collective-permute-start(f32[3,128,128]{2,1,0:T(8,128)S(1)} %get-tuple-element.113), channel_id=1, source_target_pairs={{0,96},{16,112},{32,0},{48,16},{64,32},{80,48},{96,64},{112,80},{1... | collective-permute-start | bytes 589832 | tf_op jit(solution)/shard_map/ppermute | solution.py:467
  44.2 3.1 %overflow.1 = (s32[1]{0:T(128)}, s32[513]{0:T(1024)S(1)}, f32[16,128,128]{2,1,0:T(8,128)}) custom-call(s32[2]{0:T(128)S(1)} %pad_add_fusion.me_ref, s32[40,128]{1,0:T(8,128)S(1)} %get-tuple-element.258.info_ref.refs_1_, s32[128,128]{1,0:T(8,128)S(1)} %bitcast.39, bf16[6,128,128]{2,1,0:T(8,128)(2,1)S(1)} %get-tuple-element.108.maps_ref), custom_call_target="tpu_custom_call" | custom-call | flops 1000000000 | bytes 100000 | tf_op jit(solution)/shard_map/overflow/pallas_call | solution.py:258
  47.3 0.2 collective-permute-done.15.rest_2_
  47.5 1.5 %collective-permute-start.22 = (f32[8,128,128]{2,1,0:T(8,128)S(1)}, f32[8,128,128]{2,1,0:T(8,128)}, u32[]{:S(2)}, u32[]{:S(2)}) collective-permute-start(f32[8,128,128]{2,1,0:T(8,128)S(1)} %get-tuple-element.262.rest_0_), channel_id=1, source_target_pairs={{0,1},{1,0},{2,3},{3,2},{4,5},{5,4},{6,7},{7,6},{8,9},{9,8},{10,11... | collective-permute-start | bytes 1572872 | tf_op jit(solution)/shard_map/ppermute | solution.py:479
  49.0 6.0 %collective-permute-done.19.refs_1_.rest_13_ = f32[3,128,128]{2,1,0:T(8,128)S(1)} collective-permute-done((f32[3,128,128]{2,1,0:T(8,128)S(1)}, f32[3,128,128]{2,1,0:T(8,128)S(1)}, u32[]{:S(2)}, u32[]{:S(2)}) %collective-permute-start.19) | collective-permute-done | bytes 196640 | tf_op jit(solution)/shard_map/ppermute | solution.py:467
  55.1 1.4 %collective-permute-start.23 = (f32[8,128,128]{2,1,0:T(8,128)S(1)}, f32[8,128,128]{2,1,0:T(8,128)}, u32[]{:S(2)}, u32[]{:S(2)}) collective-permute-start(f32[8,128,128]{2,1,0:T(8,128)S(1)} %hold.2.rest_1_), channel_id=1, source_target_pairs={{0,1},{1,0},{2,3},{3,2},{4,5},{5,4},{6,7},{7,6},{8,9},{9,8},{10,11... | collective-permute-start | bytes 1572872 | tf_op jit(solution)/shard_map/ppermute | solution.py:479
  56.5 0.0 collective-permute-done.20.refs_2_.rest_12_
  56.5 0.0 collective-permute-start.24
  56.5 0.0 collective-permute-done.16.refs_0_
  56.5 0.0 collective-permute-done.21.refs_3_.rest_11_
  56.5 0.6 %hold.3.rest_3_ = f32[8,128,128]{2,1,0:T(8,128)S(1)} custom-call(f32[8,128,128]{2,1,0:T(8,128)S(1)} %collective-permute-done.16.refs_0_, f32[3,128,128]{2,1,0:T(8,128)S(1)} %collective-permute-done.19.refs_1_.rest_13_, f32[3,128,128]{2,1,0:T(8,128)S(1)} %collective-permute-done.20.refs_2_.rest_12_, ...), custom_call_target="tpu_custom_call", output_to_operand_aliasing={{}: (0, {})} | custom-call | tf_op jit(solution)/shard_map/hold/pallas_call | solution.py:560
  57.2 0.6 collective-permute-start.25
  57.7 0.0 collective-permute-done.22.rest_4_
  57.7 1.1 %collective-permute-done.23.rest_5_ = f32[8,128,128]{2,1,0:T(8,128)} collective-permute-done((f32[8,128,128]{2,1,0:T(8,128)S(1)}, f32[8,128,128]{2,1,0:T(8,128)}, u32[]{:S(2)}, u32[]{:S(2)}) %collective-permute-start.23) | collective-permute-done | bytes 524320 | tf_op jit(solution)/shard_map/ppermute | solution.py:479
  58.8 0.4 collective-permute-done.24.rest_6_
  59.2 0.5 collective-permute-done.25.rest_7_
  59.7 2.9 %products.2 = f32[16,128,128]{2,1,0:T(8,128)} custom-call(s32[513]{0:T(1024)S(1)} %get-tuple-element.109.list_ref, f32[8,128,128]{2,1,0:T(8,128)S(1)} %get-tuple-element.262.rest_0_, f32[8,128,128]{2,1,0:T(8,128)S(1)} %hold.2.rest_1_, f32[8,128,128]{2,1,0:T(8,128)} %collective-permute-done.15.rest_2_, ...), custom_call_target="tpu_custom_call", output_to_operand_aliasing={{}: (15, {})} | custom-call | flops 100663296 | bytes 1572864 | tf_op jit(solution)/shard_map/products/pallas_call | solution.py:440
  62.6 0.6 %while.10 = (s32[]{:T(128)}, f32[16,128,128]{2,1,0:T(8,128)}, s32[]{:T(128)}, s32[2]{0:T(128)S(1)}, s32[40,128]{1,0:T(8,128)S(1)}, /*index=5*/f32[16,128,128]{2,...) while((s32[]{:T(128)}, f32[16,128,128]{2,1,0:T(8,128)}, ...), condition=%wide.region_1.2_spmd, body=%wide.region_0.1_spmd.sunk | while | flops 100663296 | bytes 13107597 | solution.py:645
  (20 shorter events, 0.2 us)
Async XLA Ops:
  0.0 0.7 %copy-start.3 = (s32[1,1,16]{2,1,0:T(1,128)S(1)}, s32[1,1,16]{2,1,0:T(1,128)}, u32[]{:S(2)}) copy-start(s32[1,1,16]{2,1,0:T(1,128)} %param.11) | copy-start | bytes 196
  0.0 0.7 %copy-start.1 = (s32[1,1,2,8]{3,2,1,0:T(2,128)S(1)}, s32[1,1,2,8]{3,2,1,0:T(2,128)}, u32[]{:S(2)}) copy-start(s32[1,1,2,8]{3,2,1,0:T(2,128)} %param.10) | copy-start | bytes 196
  0.0 0.7 %copy-start.2 = (s32[1,1,4]{2,1,0:T(1,128)S(1)}, s32[1,1,4]{2,1,0:T(1,128)}, u32[]{:S(2)}) copy-start(s32[1,1,4]{2,1,0:T(1,128)} %param.8) | copy-start | bytes 52
  0.7 1.0 %copy-start = (f32[1,1,4,128,128]{4,3,2,1,0:T(8,128)S(1)}, f32[1,1,4,128,128]{4,3,2,1,0:T(8,128)}, u32[]{:S(2)}) copy-start(f32[1,1,4,128,128]{4,3,2,1,0:T(8,128)} %param.7) | copy-start | bytes 786436
  2.3 9.7 %collective-permute-start.3 = (f32[4,128,128]{2,1,0:T(8,128)S(1)}, f32[4,128,128]{2,1,0:T(8,128)S(1)}, u32[]{:S(2)}, u32[]{:S(2)}) collective-permute-start(f32[4,128,128]{2,1,0:T(8,128)S(1)} %get-tuple-element.104.tile_ref), channel_id=1, source_target_pairs={{0,8},{1,9},{2,10},{3,11},{4,12},{5,13},{6,14},{7,15},{8,0},{9,1},... | collective-permute-start | bytes 786440 | tf_op jit(solution)/shard_map/ppermute | solution.py:479
  4.4 4.1 %collective-permute-start.4 = (s32[128]{0:T(128)S(1)}, s32[128]{0:T(128)S(1)}, u32[]{:S(2)}, u32[]{:S(2)}) collective-permute-start(s32[128]{0:T(128)S(1)} %bitcast.43), channel_id=1, source_target_pairs={{32,0},{33,1},{34,2},{35,3},{36,4},{37,5},{38,6},{39,7},{40,8},{41... | collective-permute-start | bytes 1544 | tf_op jit(solution)/shard_map/ppermute | solution.py:579
  5.7 5.5 %collective-permute-start.5 = (s32[128]{0:T(128)S(1)}, s32[128]{0:T(128)S(1)}, u32[]{:S(2)}, u32[]{:S(2)}) collective-permute-start(s32[128]{0:T(128)S(1)} %bitcast.44), channel_id=1, source_target_pairs={{64,0},{65,1},{66,2},{67,3},{68,4},{69,5},{70,6},{71,7},{72,8},{73... | collective-permute-start | bytes 1544 | tf_op jit(solution)/shard_map/ppermute | solution.py:579
  8.3 3.6 %collective-permute-start.6 = (s32[128]{0:T(128)S(1)}, s32[128]{0:T(128)S(1)}, u32[]{:S(2)}, u32[]{:S(2)}) collective-permute-start(s32[128]{0:T(128)S(1)} %bitcast.45), channel_id=1, source_target_pairs={{96,0},{97,1},{98,2},{99,3},{100,4},{101,5},{102,6},{103,7},{104,8... | collective-permute-start | bytes 1544 | tf_op jit(solution)/shard_map/ppermute | solution.py:579
  8.3 28.9 %copy-start.4 = (f32[1,1,2,8,128,128]{5,4,3,2,1,0:T(8,128)S(1)}, f32[1,1,2,8,128,128]{5,4,3,2,1,0:T(8,128)}, u32[]{:S(2)}) copy-start(f32[1,1,2,8,128,128]{5,4,3,2,1,0:T(8,128)} %param.9) | copy-start | bytes 3145732
  8.4 28.8 %collective-permute-start.17 = (f32[16,128,128]{2,1,0:T(8,128)}, f32[16,128,128]{2,1,0:T(8,128)}, u32[]{:S(2)}, u32[]{:S(2)}) collective-permute-start(f32[16,128,128]{2,1,0:T(8,128)} %bitcast.46), channel_id=1, source_target_pairs={{0,32},{16,48},{32,64},{48,80},{64,96},{80,112},{96,0},{112,16},{1... | collective-permute-start | bytes 3145736 | tf_op jit(solution)/shard_map/ppermute | solution.py:467
  8.5 28.8 %collective-permute-start.18 = (f32[16,128,128]{2,1,0:T(8,128)}, f32[16,128,128]{2,1,0:T(8,128)}, u32[]{:S(2)}, u32[]{:S(2)}) collective-permute-start(f32[16,128,128]{2,1,0:T(8,128)} %bitcast.47), channel_id=1, source_target_pairs={{0,96},{16,112},{32,0},{48,16},{64,32},{80,48},{96,64},{112,80},{1... | collective-permute-start | bytes 3145736 | tf_op jit(solution)/shard_map/ppermute | solution.py:467
  12.0 5.0 %collective-permute-start.7 = (s32[4,128]{1,0:T(4,128)S(1)}, s32[4,128]{1,0:T(4,128)S(1)}, u32[]{:S(2)}, u32[]{:S(2)}) collective-permute-start(s32[4,128]{1,0:T(4,128)S(1)} %get-tuple-element.106), channel_id=1, source_target_pairs={{2,0},{3,1},{0,2},{1,3},{6,4},{7,5},{4,6},{5,7},{10,8},{11,9},{8,1... | collective-permute-start | bytes 6152 | tf_op jit(solution)/shard_map/ppermute | solution.py:579
  13.7 4.3 %collective-permute-start.8 = (s32[4,128]{1,0:T(4,128)S(1)}, s32[4,128]{1,0:T(4,128)S(1)}, u32[]{:S(2)}, u32[]{:S(2)}) collective-permute-start(s32[4,128]{1,0:T(4,128)S(1)} %get-tuple-element.106), channel_id=1, source_target_pairs={{4,0},{5,1},{6,2},{7,3},{0,4},{1,5},{2,6},{3,7},{12,8},{13,9},{14,... | collective-permute-start | bytes 6152 | tf_op jit(solution)/shard_map/ppermute | solution.py:579
  17.0 4.0 %collective-permute-start.9 = (s32[4,128]{1,0:T(4,128)S(1)}, s32[4,128]{1,0:T(4,128)S(1)}, u32[]{:S(2)}, u32[]{:S(2)}) collective-permute-start(s32[4,128]{1,0:T(4,128)S(1)} %get-tuple-element.106), channel_id=1, source_target_pairs={{6,0},{7,1},{4,2},{5,3},{2,4},{3,5},{0,6},{1,7},{14,8},{15,9},{12,... | collective-permute-start | bytes 6152 | tf_op jit(solution)/shard_map/ppermute | solution.py:579
  17.1 19.4 %collective-permute-start.14 = (f32[8,128,128]{2,1,0:T(8,128)S(1)}, f32[8,128,128]{2,1,0:T(8,128)S(1)}, u32[]{:S(2)}, u32[]{:S(2)}) collective-permute-start(f32[8,128,128]{2,1,0:T(8,128)S(1)} %get-tuple-element.262.rest_0_), channel_id=1, source_target_pairs={{0,2},{1,3},{2,4},{3,5},{4,6},{5,7},{6,0},{7,1},{8,10},{9,11},{10,... | collective-permute-start | bytes 1572872 | tf_op jit(solution)/shard_map/ppermute | solution.py:479
  21.1 3.1 %collective-permute-start.10 = (s32[4,4,128]{2,1,0:T(4,128)S(1)}, s32[4,4,128]{2,1,0:T(4,128)S(1)}, u32[]{:S(2)}, u32[]{:S(2)}) collective-permute-start(s32[4,4,128]{2,1,0:T(4,128)S(1)} %constant_dynamic-update-slice_fusion), channel_id=1, source_target_pairs={{8,0},{9,1},{10,2},{11,3},{12,4},{13,5},{14,6},{15,7},{0,8},{1,9},... | collective-permute-start | bytes 24584 | tf_op jit(solution)/shard_map/ppermute | solution.py:579
  21.4 4.5 %collective-permute-start.11 = (s32[4,4,128]{2,1,0:T(4,128)S(1)}, s32[4,4,128]{2,1,0:T(4,128)S(1)}, u32[]{:S(2)}, u32[]{:S(2)}) collective-permute-start(s32[4,4,128]{2,1,0:T(4,128)S(1)} %constant_dynamic-update-slice_fusion), channel_id=1, source_target_pairs={{16,0},{17,1},{18,2},{19,3},{20,4},{21,5},{22,6},{23,7},{24,8},{25... | collective-permute-start | bytes 24584 | tf_op jit(solution)/shard_map/ppermute | solution.py:579
  24.2 4.1 %collective-permute-start.12 = (s32[4,4,128]{2,1,0:T(4,128)S(1)}, s32[4,4,128]{2,1,0:T(4,128)S(1)}, u32[]{:S(2)}, u32[]{:S(2)}) collective-permute-start(s32[4,4,128]{2,1,0:T(4,128)S(1)} %constant_dynamic-update-slice_fusion), channel_id=1, source_target_pairs={{24,0},{25,1},{26,2},{27,3},{28,4},{29,5},{30,6},{31,7},{16,8},{17... | collective-permute-start | bytes 24584 | tf_op jit(solution)/shard_map/ppermute | solution.py:579
  28.3 6.3 %collective-permute-start.13 = (s32[4,4,4,128]{3,2,1,0:T(4,128)S(1)}, s32[4,4,4,128]{3,2,1,0:T(4,128)S(1)}, u32[]{:S(2)}, u32[]{:S(2)}) collective-permute-start(s32[4,4,4,128]{3,2,1,0:T(4,128)S(1)} %bitcast_dynamic-update-slice_fusion.2), channel_id=1, source_target_pairs={{1,0},{0,1},{3,2},{2,3},{5,4},{4,5},{7,6},{6,7},{9,8},{8,9},{11,10... | collective-permute-start | bytes 98312 | tf_op jit(solution)/shard_map/ppermute | solution.py:579
  33.8 13.7 %collective-permute-start.15 = (f32[8,128,128]{2,1,0:T(8,128)S(1)}, f32[8,128,128]{2,1,0:T(8,128)}, u32[]{:S(2)}, u32[]{:S(2)}) collective-permute-start(f32[8,128,128]{2,1,0:T(8,128)S(1)} %get-tuple-element.262.rest_0_), channel_id=1, source_target_pairs={{0,6},{1,7},{2,0},{3,1},{4,2},{5,3},{6,4},{7,5},{8,14},{9,15},{10,... | collective-permute-start | bytes 1572872 | tf_op jit(solution)/shard_map/ppermute | solution.py:479
  36.5 20.0 %collective-permute-start.16 = (f32[8,128,128]{2,1,0:T(8,128)S(1)}, f32[8,128,128]{2,1,0:T(8,128)S(1)}, u32[]{:S(2)}, u32[]{:S(2)}) collective-permute-start(f32[8,128,128]{2,1,0:T(8,128)S(1)} %hold.2.rest_1_), channel_id=1, source_target_pairs={{0,2},{1,3},{2,4},{3,5},{4,6},{5,7},{6,0},{7,1},{8,10},{9,11},{10,... | collective-permute-start | bytes 1572872 | tf_op jit(solution)/shard_map/ppermute | solution.py:479
  38.8 17.7 %collective-permute-start.21 = (f32[6,128,128]{2,1,0:T(8,128)S(1)}, f32[6,128,128]{2,1,0:T(8,128)S(1)}, u32[]{:S(2)}, u32[]{:S(2)}) collective-permute-start(f32[6,128,128]{2,1,0:T(8,128)S(1)} %get-tuple-element.114), channel_id=1, source_target_pairs={{0,16},{16,0},{32,48},{48,32},{64,80},{80,64},{96,112},{112,96},{1... | collective-permute-start | bytes 1179656 | tf_op jit(solution)/shard_map/ppermute | solution.py:467
  39.4 15.7 %collective-permute-start.19 = (f32[3,128,128]{2,1,0:T(8,128)S(1)}, f32[3,128,128]{2,1,0:T(8,128)S(1)}, u32[]{:S(2)}, u32[]{:S(2)}) collective-permute-start(f32[3,128,128]{2,1,0:T(8,128)S(1)} %get-tuple-element.112), channel_id=1, source_target_pairs={{0,48},{16,32},{32,80},{48,64},{64,112},{80,96},{96,16},{112,0},{1... | collective-permute-start | bytes 589832 | tf_op jit(solution)/shard_map/ppermute | solution.py:467
  40.0 16.5 %collective-permute-start.20 = (f32[3,128,128]{2,1,0:T(8,128)S(1)}, f32[3,128,128]{2,1,0:T(8,128)S(1)}, u32[]{:S(2)}, u32[]{:S(2)}) collective-permute-start(f32[3,128,128]{2,1,0:T(8,128)S(1)} %get-tuple-element.113), channel_id=1, source_target_pairs={{0,96},{16,112},{32,0},{48,16},{64,32},{80,48},{96,64},{112,80},{1... | collective-permute-start | bytes 589832 | tf_op jit(solution)/shard_map/ppermute | solution.py:467
  47.5 10.2 %collective-permute-start.22 = (f32[8,128,128]{2,1,0:T(8,128)S(1)}, f32[8,128,128]{2,1,0:T(8,128)}, u32[]{:S(2)}, u32[]{:S(2)}) collective-permute-start(f32[8,128,128]{2,1,0:T(8,128)S(1)} %get-tuple-element.262.rest_0_), channel_id=1, source_target_pairs={{0,1},{1,0},{2,3},{3,2},{4,5},{5,4},{6,7},{7,6},{8,9},{9,8},{10,11... | collective-permute-start | bytes 1572872 | tf_op jit(solution)/shard_map/ppermute | solution.py:479
  55.1 3.8 %collective-permute-start.23 = (f32[8,128,128]{2,1,0:T(8,128)S(1)}, f32[8,128,128]{2,1,0:T(8,128)}, u32[]{:S(2)}, u32[]{:S(2)}) collective-permute-start(f32[8,128,128]{2,1,0:T(8,128)S(1)} %hold.2.rest_1_), channel_id=1, source_target_pairs={{0,1},{1,0},{2,3},{3,2},{4,5},{5,4},{6,7},{7,6},{8,9},{9,8},{10,11... | collective-permute-start | bytes 1572872 | tf_op jit(solution)/shard_map/ppermute | solution.py:479
  56.5 2.7 %collective-permute-start.24 = (f32[8,128,128]{2,1,0:T(8,128)}, f32[8,128,128]{2,1,0:T(8,128)}, u32[]{:S(2)}, u32[]{:S(2)}) collective-permute-start(f32[8,128,128]{2,1,0:T(8,128)} %collective-permute-done.15.rest_2_), channel_id=1, source_target_pairs={{0,1},{1,0},{2,3},{3,2},{4,5},{5,4},{6,7},{7,6},{8,9},{9,8},{10,11... | collective-permute-start | bytes 1572872 | tf_op jit(solution)/shard_map/ppermute | solution.py:479
  57.2 2.5 %collective-permute-start.25 = (f32[8,128,128]{2,1,0:T(8,128)S(1)}, f32[8,128,128]{2,1,0:T(8,128)}, u32[]{:S(2)}, u32[]{:S(2)}) collective-permute-start(f32[8,128,128]{2,1,0:T(8,128)S(1)} %hold.3.rest_3_), channel_id=1, source_target_pairs={{0,1},{1,0},{2,3},{3,2},{4,5},{5,4},{6,7},{7,6},{8,9},{9,8},{10,11... | collective-permute-start | bytes 1572872 | tf_op jit(solution)/shard_map/ppermute | solution.py:479

commit v2 on v0

--- a/solution.py
+++ b/solution.py
@@ -17,7 +17,7 @@
 VMEM_LIMIT = 8 << 20
 A_PARTS = 8
 LIST = 512
-AHEAD = 8
+AHEAD = 16
 
 
 def matmul(a, b):

time: 63.1 us -> 63.8 us (1.011)
  waiting for transfers between devices: 15.3 us -> 17.5 us
  starting transfers between devices: 34.3 us -> 32.3 us
    ppermute x5, waiting for transfers between devices: 4.81 us -> 7.62 us  [to_row(): return lax.ppermute(block, 'row', [(i, there(i)) for i in range(rows)])]
    ppermute x8, starting transfers between devices: 7.05 us -> 5.04 us  [moved(): return lax.ppermute(block, COL, [(i, there(i)) for i in range(columns)])]
    pallas_call x1, Pallas kernels: 0.8 us -> 1.71 us  [pack(): pl.pallas_call(functools.partial(pack_kernel, sizes), in_specs=[pl.BlockS...]
    ppermute x8, waiting for transfers between devices: 2.7 us -> 2.03 us  [moved(): return lax.ppermute(block, COL, [(i, there(i)) for i in range(columns)])]
  transfers between devices with their start and end apart: 23 -> 23, of which waited for: 10 -> 10; matrix products, arithmetic and copies ran while one was open for 1% -> 1% of each run, Pallas kernels for 10% -> 11%
where the time goes in v2:
time: 63.8 us; the launch traced here: 63.7 us
  starting transfers between devices  32.3 us (51%)
  waiting for transfers between devices  17.5 us (27%)
  Pallas kernels  10.8 us (17%)
  local copies, waits for them, and re-layouts  1.89 us (3%)
  loops' own time  0.82 us (1%)
    ppermute x10, starting transfers between devices, among(): got = lax.ppermute(held, ('row', *COL), pairs)  19.1 us
    ppermute x5, starting transfers between devices, to_row(): return lax.ppermute(block, 'row', [(i, there(i)) for i in range(rows)])  8.2 us
    ppermute x10, waiting for transfers between devices, among(): got = lax.ppermute(held, ('row', *COL), pairs)  7.81 us
    ppermute x5, waiting for transfers between devices, to_row(): return lax.ppermute(block, 'row', [(i, there(i)) for i in range(rows)])  7.62 us
    ppermute x8, starting transfers between devices, moved(): return lax.ppermute(block, COL, [(i, there(i)) for i in range(columns)])  5.04 us
    pallas_call x1, Pallas kernels, overflow(): pl.pallas_call(overflow_kernel, in_specs=[smem, vmem, vmem, vmem], out_sp...  2.98 us
    pallas_call x1, Pallas kernels, products(): pl.pallas_call(functools.partial(kernel, parts), in_specs=[smem if x.ndim...  2.97 us
    ppermute x8, waiting for transfers between devices, moved(): return lax.ppermute(block, COL, [(i, there(i)) for i in range(columns)])  2.03 us
  transfers between devices with their start and end apart: 23, of which 10 were waited for; matrix products, arithmetic and copies ran while one was open for 1% of the time, Pallas kernels for 11%

profile of v2, /device:TPU:1, one launch (start us, length us, event | category | flops | bytes accessed | tf_op | source)
XLA Modules:
  0.0 63.7 jit_solution(17657056918421189333)
XLA Ops:
  0.0 0.0 copy-start.3
  0.0 0.0 copy-start.1
  0.0 0.0 copy-start.2
  0.0 0.6 %copy-done.3 = s32[1,1,16]{2,1,0:T(1,128)S(1)} copy-done((s32[1,1,16]{2,1,0:T(1,128)S(1)}, s32[1,1,16]{2,1,0:T(1,128)}, u32[]{:S(2)}) %copy-start.3) | copy-done | bytes 88
  0.7 0.0 copy-done.1
  0.7 0.0 copy-done.2
  0.7 0.0 copy-start
  0.7 0.9 %copy-done = f32[1,1,4,128,128]{4,3,2,1,0:T(8,128)S(1)} copy-done((f32[1,1,4,128,128]{4,3,2,1,0:T(8,128)S(1)}, f32[1,1,4,128,128]{4,3,2,1,0:T(8,128)}, u32[]{:S(2)}) %copy-start) | copy-done | bytes 262168
  1.6 0.6 line.1
  2.3 2.1 %collective-permute-start.3 = (f32[4,128,128]{2,1,0:T(8,128)S(1)}, f32[4,128,128]{2,1,0:T(8,128)S(1)}, u32[]{:S(2)}, u32[]{:S(2)}) collective-permute-start(f32[4,128,128]{2,1,0:T(8,128)S(1)} %get-tuple-element.104.tile_ref), channel_id=1, source_target_pairs={{0,8},{1,9},{2,10},{3,11},{4,12},{5,13},{6,14},{7,15},{8,0},{9,1},... | collective-permute-start | bytes 786440 | tf_op jit(solution)/shard_map/ppermute | solution.py:479
  4.4 1.3 %collective-permute-start.4 = (s32[128]{0:T(128)S(1)}, s32[128]{0:T(128)S(1)}, u32[]{:S(2)}, u32[]{:S(2)}) collective-permute-start(s32[128]{0:T(128)S(1)} %bitcast.43), channel_id=1, source_target_pairs={{32,0},{33,1},{34,2},{35,3},{36,4},{37,5},{38,6},{39,7},{40,8},{41... | collective-permute-start | bytes 1544 | tf_op jit(solution)/shard_map/ppermute | solution.py:570
  5.7 2.6 %collective-permute-start.5 = (s32[128]{0:T(128)S(1)}, s32[128]{0:T(128)S(1)}, u32[]{:S(2)}, u32[]{:S(2)}) collective-permute-start(s32[128]{0:T(128)S(1)} %bitcast.44), channel_id=1, source_target_pairs={{64,0},{65,1},{66,2},{67,3},{68,4},{69,5},{70,6},{71,7},{72,8},{73... | collective-permute-start | bytes 1544 | tf_op jit(solution)/shard_map/ppermute | solution.py:570
  8.3 0.0 collective-permute-start.6
  8.3 0.1 pad_add_fusion.me_ref
  8.4 0.0 collective-permute-start.17
  8.5 0.0 collective-permute-done.4
  8.5 2.7 %collective-permute-start.18 = (f32[16,128,128]{2,1,0:T(8,128)}, f32[16,128,128]{2,1,0:T(8,128)}, u32[]{:S(2)}, u32[]{:S(2)}) collective-permute-start(f32[16,128,128]{2,1,0:T(8,128)} %bitcast.47), channel_id=1, source_target_pairs={{0,96},{16,112},{32,0},{48,16},{64,32},{80,48},{96,64},{112,80},{1... | collective-permute-start | bytes 3145736 | tf_op jit(solution)/shard_map/ppermute | solution.py:467
  11.2 0.0 collective-permute-done.5
  11.3 0.6 %collective-permute-done.6 = s32[128]{0:T(128)S(1)} collective-permute-done((s32[128]{0:T(128)S(1)}, s32[128]{0:T(128)S(1)}, u32[]{:S(2)}, u32[]{:S(2)}) %collective-permute-start.6) | collective-permute-done | bytes 544 | tf_op jit(solution)/shard_map/ppermute | solution.py:570
  11.9 0.0 collective-permute-done.3.beside_ref
  11.9 0.1 pair.1
  12.0 1.7 %collective-permute-start.7 = (s32[4,128]{1,0:T(4,128)S(1)}, s32[4,128]{1,0:T(4,128)S(1)}, u32[]{:S(2)}, u32[]{:S(2)}) collective-permute-start(s32[4,128]{1,0:T(4,128)S(1)} %get-tuple-element.106), channel_id=1, source_target_pairs={{2,0},{3,1},{0,2},{1,3},{6,4},{7,5},{4,6},{5,7},{10,8},{11,9},{8,1... | collective-permute-start | bytes 6152 | tf_op jit(solution)/shard_map/ppermute | solution.py:570
  13.7 3.3 %collective-permute-start.8 = (s32[4,128]{1,0:T(4,128)S(1)}, s32[4,128]{1,0:T(4,128)S(1)}, u32[]{:S(2)}, u32[]{:S(2)}) collective-permute-start(s32[4,128]{1,0:T(4,128)S(1)} %get-tuple-element.106), channel_id=1, source_target_pairs={{4,0},{5,1},{6,2},{7,3},{0,4},{1,5},{2,6},{3,7},{12,8},{13,9},{14,... | collective-permute-start | bytes 6152 | tf_op jit(solution)/shard_map/ppermute | solution.py:570
  17.0 0.0 collective-permute-start.9
  17.0 0.0 collective-permute-done.7
  17.1 0.1 collective-permute-start.14
  17.2 0.9 %collective-permute-done.8 = s32[4,128]{1,0:T(4,128)S(1)} collective-permute-done((s32[4,128]{1,0:T(4,128)S(1)}, s32[4,128]{1,0:T(4,128)S(1)}, u32[]{:S(2)}, u32[]{:S(2)}) %collective-permute-start.8) | collective-permute-done | bytes 2080 | tf_op jit(solution)/shard_map/ppermute | solution.py:570
  18.0 3.1 %collective-permute-done.9 = s32[4,128]{1,0:T(4,128)S(1)} collective-permute-done((s32[4,128]{1,0:T(4,128)S(1)}, s32[4,128]{1,0:T(4,128)S(1)}, u32[]{:S(2)}, u32[]{:S(2)}) %collective-permute-start.9) | collective-permute-done | bytes 2080 | tf_op jit(solution)/shard_map/ppermute | solution.py:570
  21.1 0.3 collective-permute-start.10
  21.4 2.8 %collective-permute-start.11 = (s32[4,4,128]{2,1,0:T(4,128)S(1)}, s32[4,4,128]{2,1,0:T(4,128)S(1)}, u32[]{:S(2)}, u32[]{:S(2)}) collective-permute-start(s32[4,4,128]{2,1,0:T(4,128)S(1)} %constant_dynamic-update-slice_fusion), channel_id=1, source_target_pairs={{16,0},{17,1},{18,2},{19,3},{20,4},{21,5},{22,6},{23,7},{24,8},{25... | collective-permute-start | bytes 24584 | tf_op jit(solution)/shard_map/ppermute | solution.py:570
  24.2 0.0 collective-permute-done.10
  24.2 1.6 %collective-permute-start.12 = (s32[4,4,128]{2,1,0:T(4,128)S(1)}, s32[4,4,128]{2,1,0:T(4,128)S(1)}, u32[]{:S(2)}, u32[]{:S(2)}) collective-permute-start(s32[4,4,128]{2,1,0:T(4,128)S(1)} %constant_dynamic-update-slice_fusion), channel_id=1, source_target_pairs={{24,0},{25,1},{26,2},{27,3},{28,4},{29,5},{30,6},{31,7},{16,8},{17... | collective-permute-start | bytes 24584 | tf_op jit(solution)/shard_map/ppermute | solution.py:570
  25.8 0.0 collective-permute-done.11
  25.8 2.5 %collective-permute-done.12 = s32[4,4,128]{2,1,0:T(4,128)S(1)} collective-permute-done((s32[4,4,128]{2,1,0:T(4,128)S(1)}, s32[4,4,128]{2,1,0:T(4,128)S(1)}, u32[]{:S(2)}, u32[]{:S(2)}) %collective-permute-start.12) | collective-permute-done | bytes 8224 | tf_op jit(solution)/shard_map/ppermute | solution.py:570
  28.3 5.4 %collective-permute-start.13 = (s32[4,4,4,128]{3,2,1,0:T(4,128)S(1)}, s32[4,4,4,128]{3,2,1,0:T(4,128)S(1)}, u32[]{:S(2)}, u32[]{:S(2)}) collective-permute-start(s32[4,4,4,128]{3,2,1,0:T(4,128)S(1)} %bitcast_dynamic-update-slice_fusion.2), channel_id=1, source_target_pairs={{1,0},{0,1},{3,2},{2,3},{5,4},{4,5},{7,6},{6,7},{9,8},{8,9},{11,10... | collective-permute-start | bytes 98312 | tf_op jit(solution)/shard_map/ppermute | solution.py:570
  33.8 0.1 collective-permute-start.15
  33.9 0.7 %collective-permute-done.13 = s32[4,4,4,128]{3,2,1,0:T(4,128)S(1)} collective-permute-done((s32[4,4,4,128]{3,2,1,0:T(4,128)S(1)}, s32[4,4,4,128]{3,2,1,0:T(4,128)S(1)}, u32[]{:S(2)}, u32[]{:S(2)}) %collective-permute-start.13) | collective-permute-done | bytes 32800 | tf_op jit(solution)/shard_map/ppermute | solution.py:570
  34.6 1.8 %plan.1 = (s32[12]{0:T(128)S(1)}, s32[40,128]{1,0:T(8,128)S(1)}, bf16[6,128,128]{2,1,0:T(8,128)(2,1)S(1)}) custom-call(s32[2]{0:T(128)S(1)} %pad_add_fusion.me_ref, s32[128,128]{1,0:T(8,128)S(1)} %bitcast.38), custom_call_target="tpu_custom_call" | custom-call | tf_op jit(solution)/shard_map/plan/pallas_call | solution.py:178
  36.4 0.0 collective-permute-done.14.refs_0_
  36.5 0.8 %collective-permute-start.16 = (f32[8,128,128]{2,1,0:T(8,128)S(1)}, f32[8,128,128]{2,1,0:T(8,128)S(1)}, u32[]{:S(2)}, u32[]{:S(2)}) collective-permute-start(f32[8,128,128]{2,1,0:T(8,128)S(1)} %hold.2.rest_1_), channel_id=1, source_target_pairs={{0,2},{1,3},{2,4},{3,5},{4,6},{5,7},{6,0},{7,1},{8,10},{9,11},{10,... | collective-permute-start | bytes 1572872 | tf_op jit(solution)/shard_map/ppermute | solution.py:479
  37.2 0.0 collective-permute-done.17.rest_1_.rest_9_
  37.3 0.0 collective-permute-done.18.rest_2_.rest_10_
  37.3 0.0 copy-done.4
  37.3 1.7 %pack.2 = (f32[3,128,128]{2,1,0:T(8,128)S(1)}, f32[3,128,128]{2,1,0:T(8,128)S(1)}, f32[6,128,128]{2,1,0:T(8,128)S(1)}) custom-call(s32[12]{0:T(128)S(1)} %get-tuple-element.111.list_ref, f32[16,128,128]{2,1,0:T(8,128)S(1)} %bitcast.48, f32[16,128,128]{2,1,0:T(8,128)} %collective-permute-done.17.rest_1_.rest_9_, ...), custom_call_target="tpu_custom_call" | custom-call | tf_op jit(solution)/shard_map/pack/pallas_call | solution.py:211
  39.0 1.2 %collective-permute-start.21 = (f32[6,128,128]{2,1,0:T(8,128)S(1)}, f32[6,128,128]{2,1,0:T(8,128)S(1)}, u32[]{:S(2)}, u32[]{:S(2)}) collective-permute-start(f32[6,128,128]{2,1,0:T(8,128)S(1)} %get-tuple-element.114), channel_id=1, source_target_pairs={{0,16},{16,0},{32,48},{48,32},{64,80},{80,64},{96,112},{112,96},{1... | collective-permute-start | bytes 1179656 | tf_op jit(solution)/shard_map/ppermute | solution.py:467
  40.1 0.6 collective-permute-start.19
  40.8 3.7 %collective-permute-start.20 = (f32[3,128,128]{2,1,0:T(8,128)S(1)}, f32[3,128,128]{2,1,0:T(8,128)S(1)}, u32[]{:S(2)}, u32[]{:S(2)}) collective-permute-start(f32[3,128,128]{2,1,0:T(8,128)S(1)} %get-tuple-element.113), channel_id=1, source_target_pairs={{0,96},{16,112},{32,0},{48,16},{64,32},{80,48},{96,64},{112,80},{1... | collective-permute-start | bytes 589832 | tf_op jit(solution)/shard_map/ppermute | solution.py:467
  44.4 3.0 %overflow.1 = (s32[1]{0:T(128)}, s32[513]{0:T(1024)S(1)}, f32[16,128,128]{2,1,0:T(8,128)}) custom-call(s32[2]{0:T(128)S(1)} %pad_add_fusion.me_ref, s32[40,128]{1,0:T(8,128)S(1)} %get-tuple-element.258.info_ref.refs_1_, s32[128,128]{1,0:T(8,128)S(1)} %bitcast.39, bf16[6,128,128]{2,1,0:T(8,128)(2,1)S(1)} %get-tuple-element.108.maps_ref), custom_call_target="tpu_custom_call" | custom-call | flops 1000000000 | bytes 100000 | tf_op jit(solution)/shard_map/overflow/pallas_call | solution.py:258
  47.4 0.1 collective-permute-done.15.rest_2_
  47.5 0.8 %collective-permute-start.22 = (f32[8,128,128]{2,1,0:T(8,128)S(1)}, f32[8,128,128]{2,1,0:T(8,128)}, u32[]{:S(2)}, u32[]{:S(2)}) collective-permute-start(f32[8,128,128]{2,1,0:T(8,128)S(1)} %get-tuple-element.262.rest_0_), channel_id=1, source_target_pairs={{0,1},{1,0},{2,3},{3,2},{4,5},{5,4},{6,7},{7,6},{8,9},{9,8},{10,11... | collective-permute-start | bytes 1572872 | tf_op jit(solution)/shard_map/ppermute | solution.py:479
  48.3 7.6 %collective-permute-done.19.refs_1_.rest_13_ = f32[3,128,128]{2,1,0:T(8,128)S(1)} collective-permute-done((f32[3,128,128]{2,1,0:T(8,128)S(1)}, f32[3,128,128]{2,1,0:T(8,128)S(1)}, u32[]{:S(2)}, u32[]{:S(2)}) %collective-permute-start.19) | collective-permute-done | bytes 196640 | tf_op jit(solution)/shard_map/ppermute | solution.py:467
  55.9 0.6 collective-permute-start.23
  56.5 0.0 collective-permute-done.20.refs_2_.rest_12_
  56.5 0.0 collective-permute-start.24
  56.5 0.0 collective-permute-done.16.refs_0_
  56.5 0.0 collective-permute-done.21.refs_3_.rest_11_
  56.6 0.6 hold.3.rest_3_
  57.2 0.6 collective-permute-start.25
  57.8 0.0 collective-permute-done.22.rest_4_
  57.8 1.1 %collective-permute-done.23.rest_5_ = f32[8,128,128]{2,1,0:T(8,128)} collective-permute-done((f32[8,128,128]{2,1,0:T(8,128)S(1)}, f32[8,128,128]{2,1,0:T(8,128)}, u32[]{:S(2)}, u32[]{:S(2)}) %collective-permute-start.23) | collective-permute-done | bytes 524320 | tf_op jit(solution)/shard_map/ppermute | solution.py:479
  58.9 0.4 collective-permute-done.24.rest_6_
  59.2 0.5 collective-permute-done.25.rest_7_
  59.7 3.0 %products.2 = f32[16,128,128]{2,1,0:T(8,128)} custom-call(s32[513]{0:T(1024)S(1)} %get-tuple-element.109.list_ref, f32[8,128,128]{2,1,0:T(8,128)S(1)} %get-tuple-element.262.rest_0_, f32[8,128,128]{2,1,0:T(8,128)S(1)} %hold.2.rest_1_, f32[8,128,128]{2,1,0:T(8,128)} %collective-permute-done.15.rest_2_, ...), custom_call_target="tpu_custom_call", output_to_operand_aliasing={{}: (15, {})} | custom-call | flops 100663296 | bytes 1572864 | tf_op jit(solution)/shard_map/products/pallas_call | solution.py:440
  62.7 0.8 %while.10 = (s32[]{:T(128)}, f32[16,128,128]{2,1,0:T(8,128)}, s32[]{:T(128)}, s32[2]{0:T(128)S(1)}, s32[40,128]{1,0:T(8,128)S(1)}, /*index=5*/f32[16,128,128]{2,...) while((s32[]{:T(128)}, f32[16,128,128]{2,1,0:T(8,128)}, ...), condition=%wide.region_1.2_spmd, body=%wide.region_0.1_spmd.sunk | while | flops 100663296 | bytes 13107597 | solution.py:636
  (20 shorter events, 0.2 us)
Async XLA Ops:
  0.0 0.7 %copy-start.3 = (s32[1,1,16]{2,1,0:T(1,128)S(1)}, s32[1,1,16]{2,1,0:T(1,128)}, u32[]{:S(2)}) copy-start(s32[1,1,16]{2,1,0:T(1,128)} %param.11) | copy-start | bytes 196
  0.0 0.7 %copy-start.1 = (s32[1,1,2,8]{3,2,1,0:T(2,128)S(1)}, s32[1,1,2,8]{3,2,1,0:T(2,128)}, u32[]{:S(2)}) copy-start(s32[1,1,2,8]{3,2,1,0:T(2,128)} %param.10) | copy-start | bytes 196
  0.0 0.7 %copy-start.2 = (s32[1,1,4]{2,1,0:T(1,128)S(1)}, s32[1,1,4]{2,1,0:T(1,128)}, u32[]{:S(2)}) copy-start(s32[1,1,4]{2,1,0:T(1,128)} %param.8) | copy-start | bytes 52
  0.7 1.0 %copy-start = (f32[1,1,4,128,128]{4,3,2,1,0:T(8,128)S(1)}, f32[1,1,4,128,128]{4,3,2,1,0:T(8,128)}, u32[]{:S(2)}) copy-start(f32[1,1,4,128,128]{4,3,2,1,0:T(8,128)} %param.7) | copy-start | bytes 786436
  2.3 9.7 %collective-permute-start.3 = (f32[4,128,128]{2,1,0:T(8,128)S(1)}, f32[4,128,128]{2,1,0:T(8,128)S(1)}, u32[]{:S(2)}, u32[]{:S(2)}) collective-permute-start(f32[4,128,128]{2,1,0:T(8,128)S(1)} %get-tuple-element.104.tile_ref), channel_id=1, source_target_pairs={{0,8},{1,9},{2,10},{3,11},{4,12},{5,13},{6,14},{7,15},{8,0},{9,1},... | collective-permute-start | bytes 786440 | tf_op jit(solution)/shard_map/ppermute | solution.py:479
  4.4 4.1 %collective-permute-start.4 = (s32[128]{0:T(128)S(1)}, s32[128]{0:T(128)S(1)}, u32[]{:S(2)}, u32[]{:S(2)}) collective-permute-start(s32[128]{0:T(128)S(1)} %bitcast.43), channel_id=1, source_target_pairs={{32,0},{33,1},{34,2},{35,3},{36,4},{37,5},{38,6},{39,7},{40,8},{41... | collective-permute-start | bytes 1544 | tf_op jit(solution)/shard_map/ppermute | solution.py:570
  5.7 5.5 %collective-permute-start.5 = (s32[128]{0:T(128)S(1)}, s32[128]{0:T(128)S(1)}, u32[]{:S(2)}, u32[]{:S(2)}) collective-permute-start(s32[128]{0:T(128)S(1)} %bitcast.44), channel_id=1, source_target_pairs={{64,0},{65,1},{66,2},{67,3},{68,4},{69,5},{70,6},{71,7},{72,8},{73... | collective-permute-start | bytes 1544 | tf_op jit(solution)/shard_map/ppermute | solution.py:570
  8.3 3.6 %collective-permute-start.6 = (s32[128]{0:T(128)S(1)}, s32[128]{0:T(128)S(1)}, u32[]{:S(2)}, u32[]{:S(2)}) collective-permute-start(s32[128]{0:T(128)S(1)} %bitcast.45), channel_id=1, source_target_pairs={{96,0},{97,1},{98,2},{99,3},{100,4},{101,5},{102,6},{103,7},{104,8... | collective-permute-start | bytes 1544 | tf_op jit(solution)/shard_map/ppermute | solution.py:570
  8.3 28.9 %copy-start.4 = (f32[1,1,2,8,128,128]{5,4,3,2,1,0:T(8,128)S(1)}, f32[1,1,2,8,128,128]{5,4,3,2,1,0:T(8,128)}, u32[]{:S(2)}) copy-start(f32[1,1,2,8,128,128]{5,4,3,2,1,0:T(8,128)} %param.9) | copy-start | bytes 3145732
  8.4 28.8 %collective-permute-start.17 = (f32[16,128,128]{2,1,0:T(8,128)}, f32[16,128,128]{2,1,0:T(8,128)}, u32[]{:S(2)}, u32[]{:S(2)}) collective-permute-start(f32[16,128,128]{2,1,0:T(8,128)} %bitcast.46), channel_id=1, source_target_pairs={{0,32},{16,48},{32,64},{48,80},{64,96},{80,112},{96,0},{112,16},{1... | collective-permute-start | bytes 3145736 | tf_op jit(solution)/shard_map/ppermute | solution.py:467
  8.5 28.8 %collective-permute-start.18 = (f32[16,128,128]{2,1,0:T(8,128)}, f32[16,128,128]{2,1,0:T(8,128)}, u32[]{:S(2)}, u32[]{:S(2)}) collective-permute-start(f32[16,128,128]{2,1,0:T(8,128)} %bitcast.47), channel_id=1, source_target_pairs={{0,96},{16,112},{32,0},{48,16},{64,32},{80,48},{96,64},{112,80},{1... | collective-permute-start | bytes 3145736 | tf_op jit(solution)/shard_map/ppermute | solution.py:467
  12.0 5.0 %collective-permute-start.7 = (s32[4,128]{1,0:T(4,128)S(1)}, s32[4,128]{1,0:T(4,128)S(1)}, u32[]{:S(2)}, u32[]{:S(2)}) collective-permute-start(s32[4,128]{1,0:T(4,128)S(1)} %get-tuple-element.106), channel_id=1, source_target_pairs={{2,0},{3,1},{0,2},{1,3},{6,4},{7,5},{4,6},{5,7},{10,8},{11,9},{8,1... | collective-permute-start | bytes 6152 | tf_op jit(solution)/shard_map/ppermute | solution.py:570
  13.7 4.3 %collective-permute-start.8 = (s32[4,128]{1,0:T(4,128)S(1)}, s32[4,128]{1,0:T(4,128)S(1)}, u32[]{:S(2)}, u32[]{:S(2)}) collective-permute-start(s32[4,128]{1,0:T(4,128)S(1)} %get-tuple-element.106), channel_id=1, source_target_pairs={{4,0},{5,1},{6,2},{7,3},{0,4},{1,5},{2,6},{3,7},{12,8},{13,9},{14,... | collective-permute-start | bytes 6152 | tf_op jit(solution)/shard_map/ppermute | solution.py:570
  17.0 4.0 %collective-permute-start.9 = (s32[4,128]{1,0:T(4,128)S(1)}, s32[4,128]{1,0:T(4,128)S(1)}, u32[]{:S(2)}, u32[]{:S(2)}) collective-permute-start(s32[4,128]{1,0:T(4,128)S(1)} %get-tuple-element.106), channel_id=1, source_target_pairs={{6,0},{7,1},{4,2},{5,3},{2,4},{3,5},{0,6},{1,7},{14,8},{15,9},{12,... | collective-permute-start | bytes 6152 | tf_op jit(solution)/shard_map/ppermute | solution.py:570
  17.1 19.4 %collective-permute-start.14 = (f32[8,128,128]{2,1,0:T(8,128)S(1)}, f32[8,128,128]{2,1,0:T(8,128)S(1)}, u32[]{:S(2)}, u32[]{:S(2)}) collective-permute-start(f32[8,128,128]{2,1,0:T(8,128)S(1)} %get-tuple-element.262.rest_0_), channel_id=1, source_target_pairs={{0,2},{1,3},{2,4},{3,5},{4,6},{5,7},{6,0},{7,1},{8,10},{9,11},{10,... | collective-permute-start | bytes 1572872 | tf_op jit(solution)/shard_map/ppermute | solution.py:479
  21.1 3.1 %collective-permute-start.10 = (s32[4,4,128]{2,1,0:T(4,128)S(1)}, s32[4,4,128]{2,1,0:T(4,128)S(1)}, u32[]{:S(2)}, u32[]{:S(2)}) collective-permute-start(s32[4,4,128]{2,1,0:T(4,128)S(1)} %constant_dynamic-update-slice_fusion), channel_id=1, source_target_pairs={{8,0},{9,1},{10,2},{11,3},{12,4},{13,5},{14,6},{15,7},{0,8},{1,9},... | collective-permute-start | bytes 24584 | tf_op jit(solution)/shard_map/ppermute | solution.py:570
  21.4 4.5 %collective-permute-start.11 = (s32[4,4,128]{2,1,0:T(4,128)S(1)}, s32[4,4,128]{2,1,0:T(4,128)S(1)}, u32[]{:S(2)}, u32[]{:S(2)}) collective-permute-start(s32[4,4,128]{2,1,0:T(4,128)S(1)} %constant_dynamic-update-slice_fusion), channel_id=1, source_target_pairs={{16,0},{17,1},{18,2},{19,3},{20,4},{21,5},{22,6},{23,7},{24,8},{25... | collective-permute-start | bytes 24584 | tf_op jit(solution)/shard_map/ppermute | solution.py:570
  24.2 4.1 %collective-permute-start.12 = (s32[4,4,128]{2,1,0:T(4,128)S(1)}, s32[4,4,128]{2,1,0:T(4,128)S(1)}, u32[]{:S(2)}, u32[]{:S(2)}) collective-permute-start(s32[4,4,128]{2,1,0:T(4,128)S(1)} %constant_dynamic-update-slice_fusion), channel_id=1, source_target_pairs={{24,0},{25,1},{26,2},{27,3},{28,4},{29,5},{30,6},{31,7},{16,8},{17... | collective-permute-start | bytes 24584 | tf_op jit(solution)/shard_map/ppermute | solution.py:570
  28.3 6.3 %collective-permute-start.13 = (s32[4,4,4,128]{3,2,1,0:T(4,128)S(1)}, s32[4,4,4,128]{3,2,1,0:T(4,128)S(1)}, u32[]{:S(2)}, u32[]{:S(2)}) collective-permute-start(s32[4,4,4,128]{3,2,1,0:T(4,128)S(1)} %bitcast_dynamic-update-slice_fusion.2), channel_id=1, source_target_pairs={{1,0},{0,1},{3,2},{2,3},{5,4},{4,5},{7,6},{6,7},{9,8},{8,9},{11,10... | collective-permute-start | bytes 98312 | tf_op jit(solution)/shard_map/ppermute | solution.py:570
  33.8 13.7 %collective-permute-start.15 = (f32[8,128,128]{2,1,0:T(8,128)S(1)}, f32[8,128,128]{2,1,0:T(8,128)}, u32[]{:S(2)}, u32[]{:S(2)}) collective-permute-start(f32[8,128,128]{2,1,0:T(8,128)S(1)} %get-tuple-element.262.rest_0_), channel_id=1, source_target_pairs={{0,6},{1,7},{2,0},{3,1},{4,2},{5,3},{6,4},{7,5},{8,14},{9,15},{10,... | collective-permute-start | bytes 1572872 | tf_op jit(solution)/shard_map/ppermute | solution.py:479
  36.5 20.1 %collective-permute-start.16 = (f32[8,128,128]{2,1,0:T(8,128)S(1)}, f32[8,128,128]{2,1,0:T(8,128)S(1)}, u32[]{:S(2)}, u32[]{:S(2)}) collective-permute-start(f32[8,128,128]{2,1,0:T(8,128)S(1)} %hold.2.rest_1_), channel_id=1, source_target_pairs={{0,2},{1,3},{2,4},{3,5},{4,6},{5,7},{6,0},{7,1},{8,10},{9,11},{10,... | collective-permute-start | bytes 1572872 | tf_op jit(solution)/shard_map/ppermute | solution.py:479
  39.0 17.6 %collective-permute-start.21 = (f32[6,128,128]{2,1,0:T(8,128)S(1)}, f32[6,128,128]{2,1,0:T(8,128)S(1)}, u32[]{:S(2)}, u32[]{:S(2)}) collective-permute-start(f32[6,128,128]{2,1,0:T(8,128)S(1)} %get-tuple-element.114), channel_id=1, source_target_pairs={{0,16},{16,0},{32,48},{48,32},{64,80},{80,64},{96,112},{112,96},{1... | collective-permute-start | bytes 1179656 | tf_op jit(solution)/shard_map/ppermute | solution.py:467
  40.1 15.8 %collective-permute-start.19 = (f32[3,128,128]{2,1,0:T(8,128)S(1)}, f32[3,128,128]{2,1,0:T(8,128)S(1)}, u32[]{:S(2)}, u32[]{:S(2)}) collective-permute-start(f32[3,128,128]{2,1,0:T(8,128)S(1)} %get-tuple-element.112), channel_id=1, source_target_pairs={{0,48},{16,32},{32,80},{48,64},{64,112},{80,96},{96,16},{112,0},{1... | collective-permute-start | bytes 589832 | tf_op jit(solution)/shard_map/ppermute | solution.py:467
  40.8 15.8 %collective-permute-start.20 = (f32[3,128,128]{2,1,0:T(8,128)S(1)}, f32[3,128,128]{2,1,0:T(8,128)S(1)}, u32[]{:S(2)}, u32[]{:S(2)}) collective-permute-start(f32[3,128,128]{2,1,0:T(8,128)S(1)} %get-tuple-element.113), channel_id=1, source_target_pairs={{0,96},{16,112},{32,0},{48,16},{64,32},{80,48},{96,64},{112,80},{1... | collective-permute-start | bytes 589832 | tf_op jit(solution)/shard_map/ppermute | solution.py:467
  47.5 10.3 %collective-permute-start.22 = (f32[8,128,128]{2,1,0:T(8,128)S(1)}, f32[8,128,128]{2,1,0:T(8,128)}, u32[]{:S(2)}, u32[]{:S(2)}) collective-permute-start(f32[8,128,128]{2,1,0:T(8,128)S(1)} %get-tuple-element.262.rest_0_), channel_id=1, source_target_pairs={{0,1},{1,0},{2,3},{3,2},{4,5},{5,4},{6,7},{7,6},{8,9},{9,8},{10,11... | collective-permute-start | bytes 1572872 | tf_op jit(solution)/shard_map/ppermute | solution.py:479
  55.9 3.0 %collective-permute-start.23 = (f32[8,128,128]{2,1,0:T(8,128)S(1)}, f32[8,128,128]{2,1,0:T(8,128)}, u32[]{:S(2)}, u32[]{:S(2)}) collective-permute-start(f32[8,128,128]{2,1,0:T(8,128)S(1)} %hold.2.rest_1_), channel_id=1, source_target_pairs={{0,1},{1,0},{2,3},{3,2},{4,5},{5,4},{6,7},{7,6},{8,9},{9,8},{10,11... | collective-permute-start | bytes 1572872 | tf_op jit(solution)/shard_map/ppermute | solution.py:479
  56.5 2.7 %collective-permute-start.24 = (f32[8,128,128]{2,1,0:T(8,128)}, f32[8,128,128]{2,1,0:T(8,128)}, u32[]{:S(2)}, u32[]{:S(2)}) collective-permute-start(f32[8,128,128]{2,1,0:T(8,128)} %collective-permute-done.15.rest_2_), channel_id=1, source_target_pairs={{0,1},{1,0},{2,3},{3,2},{4,5},{5,4},{6,7},{7,6},{8,9},{9,8},{10,11... | collective-permute-start | bytes 1572872 | tf_op jit(solution)/shard_map/ppermute | solution.py:479
  57.2 2.5 %collective-permute-start.25 = (f32[8,128,128]{2,1,0:T(8,128)S(1)}, f32[8,128,128]{2,1,0:T(8,128)}, u32[]{:S(2)}, u32[]{:S(2)}) collective-permute-start(f32[8,128,128]{2,1,0:T(8,128)S(1)} %hold.3.rest_3_), channel_id=1, source_target_pairs={{0,1},{1,0},{2,3},{3,2},{4,5},{5,4},{6,7},{7,6},{8,9},{9,8},{10,11... | collective-permute-start | bytes 1572872 | tf_op jit(solution)/shard_map/ppermute | solution.py:479
